TPU v7x, 32 devices: a whole 2x2x4 slice. The times are simulated.
32 devices in a mesh: section: 2 (over y), fsdp: 16 (over z, x, core).
Axes of the slice: x: 2, y: 2, z: 4, core: 2. Of those that a mesh axis runs over, the one named last changes fastest.
Arguments:
- ends: bfloat16 [2, 2, 16, 256, 768], P('section', None, 'fsdp'), may hold values from -6 to 6
- lengths: int32 [2, 16], P(None, 'fsdp'), may hold values from 1 to 256, 2560 in all within a row
- w_qkv: bfloat16 [2, 768, 2304], P('section', 'fsdp'), as said below
- w_out: bfloat16 [2, 768, 768], P('section', 'fsdp'), may hold values from -0.4375 to 0.4375
- w_up: bfloat16 [2, 768, 3072], P('section', 'fsdp'), may hold values from -0.21875 to 0.21875
- w_down: bfloat16 [2, 3072, 768], P('section', 'fsdp'), may hold values from -0.109375 to 0.109375
- vectors: bfloat16 [2, 9216], P('section', 'fsdp')
Outputs:
- ends_out: float32 [2, 2, 16, 256, 768], P('section', None, 'fsdp')
- grad_w_qkv: float32 [2, 768, 2304], P('section', 'fsdp')
- grad_w_out: float32 [2, 768, 768], P('section', 'fsdp')
- grad_w_up: float32 [2, 768, 3072], P('section', 'fsdp')
- grad_w_down: float32 [2, 3072, 768], P('section', 'fsdp')
- grad_vectors: float32 [2, 9216], P('section', 'fsdp')
Inputs may be any that keep to these rules, and one draw needn't show every extreme that they name: Sequence s of micro-batch m is its first lengths[m, s] positions, the rest is padding; in each micro-batch the 16 lengths sum to 2560 and the longest is 256. `w_qkv`: columns 0 to 767 are the query projection, 768 to 1535 the key projection, the rest the value projection.
All inputs are finite; a program needn't handle non-finite values. No bound on the sum of `lengths` on one device may be relied on, other than what follows from the above.
Results may differ from a plain program's by a relative error of at most 0.014.
Values may be sent and summed in bfloat16 or wider, within the bound.
A program may use at most 192 MiB of HBM per device.

v0:
```python
import jax
import jax.numpy as jnp
from jax import lax
from jax.sharding import PartitionSpec as P

D = 768
HEADS = 12
FF = 3072
HEAD = 64


def shifted(value, axis, steps):
    count = lax.axis_size(axis)
    first, last = (max(0, -steps), min(count, count - steps))
    return lax.ppermute(value, axis, [(source, source + steps) for source in range(first, last)])


def split_vector(vec):
    flat_vec = vec.astype(jnp.float32)
    widths = [D, D, D, D, D, FF, D, D, D]
    pieces = []
    offset = 0
    for width in widths:
        pieces.append(flat_vec[offset : offset + width])
        offset = offset + width
    return tuple(pieces)


def normalize(hidden):
    mean_row = jnp.mean(hidden, axis=-1, keepdims=True)
    centred = hidden - mean_row
    variance = jnp.mean(centred * centred, axis=-1, keepdims=True)
    inv_std = lax.rsqrt(variance + 1e-12)
    return (centred * inv_std, inv_std)


def norm_back(grad_n, normed, inv_std):
    return inv_std * (
        grad_n
        - jnp.mean(grad_n, axis=-1, keepdims=True)
        - normed * jnp.mean(grad_n * normed, axis=-1, keepdims=True)
    )


def gelu_value(up_in):
    return 0.5 * up_in * (1.0 + lax.erf(up_in * 0.7071067811865476))


def gelu_slope(up_in):
    return (
        0.5 * (1.0 + lax.erf(up_in * 0.7071067811865476))
        + up_in * jnp.exp(-0.5 * up_in * up_in) * 0.3989422804014327
    )


def left_dot(left, right):
    return lax.dot_general(
        left, right, (((0,), (0,)), ((), ())), preferred_element_type=jnp.float32
    )


def right_dot(left, right):
    return lax.dot_general(
        left, right, (((1,), (1,)), ((), ())), preferred_element_type=jnp.float32
    )


def heads_of(matrix):
    return matrix.reshape(matrix.shape[0], HEADS, HEAD)


def scores_of(query_b, key_b, visible):
    scores = jnp.einsum(
        "qhd,khd->hqk", heads_of(query_b), heads_of(key_b), preferred_element_type=jnp.float32
    ) * HEAD ** (-0.5)
    return jnp.where(visible[None, None, :], scores, -1e30)


def attend(query_b, key_b, value_b, visible):
    row_count = query_b.shape[0]
    masked = scores_of(query_b, key_b, visible)
    row_peak = jnp.max(masked, axis=-1, keepdims=True)
    log_total = row_peak + jnp.log(jnp.sum(jnp.exp(masked - row_peak), axis=-1, keepdims=True))
    attn_probs = jnp.where(visible[None, None, :], jnp.exp(masked - log_total), 0.0)
    probs_b = attn_probs.astype(jnp.bfloat16)
    context = jnp.einsum(
        "hqk,khd->qhd", probs_b, heads_of(value_b), preferred_element_type=jnp.float32
    )
    return (log_total, context.reshape(row_count, D))


def attend_back(grad_ctx_b, query_b, key_b, value_b, log_total, context, visible):
    row_count = query_b.shape[0]
    masked = scores_of(query_b, key_b, visible)
    attn_probs = jnp.where(visible[None, None, :], jnp.exp(masked - log_total), 0.0)
    probs_b = attn_probs.astype(jnp.bfloat16)
    grad_heads = heads_of(grad_ctx_b)
    grad_v = jnp.einsum("hqk,qhd->khd", probs_b, grad_heads, preferred_element_type=jnp.float32)
    grad_p = jnp.einsum(
        "qhd,khd->hqk", grad_heads, heads_of(value_b), preferred_element_type=jnp.float32
    )
    delta_rows = jnp.sum(
        grad_heads.astype(jnp.float32) * context.reshape(row_count, HEADS, HEAD), axis=-1
    )
    grad_s = attn_probs * (grad_p - jnp.transpose(delta_rows)[:, :, None]) * HEAD ** (-0.5)
    grad_s_b = grad_s.astype(jnp.bfloat16)
    grad_q = jnp.einsum(
        "hqk,khd->qhd", grad_s_b, heads_of(key_b), preferred_element_type=jnp.float32
    )
    grad_k = jnp.einsum(
        "hqk,qhd->khd", grad_s_b, heads_of(query_b), preferred_element_type=jnp.float32
    )
    return jnp.concatenate(
        [grad_q.reshape(row_count, D), grad_k.reshape(row_count, D), grad_v.reshape(row_count, D)],
        axis=1,
    )


def layer_forward(x_in, visible, params):
    w_qkv, w_out, w_up, w_down, vec = params
    bias_q, bias_v, bias_o, gain1, shift1, bias_up, bias_down, gain2, shift2 = split_vector(vec)
    projected = jnp.dot(x_in, w_qkv, preferred_element_type=jnp.float32)
    query_b = (projected[:, :D] + bias_q).astype(jnp.bfloat16)
    key_b = projected[:, D : 2 * D].astype(jnp.bfloat16)
    value_b = (projected[:, 2 * D :] + bias_v).astype(jnp.bfloat16)
    log_total, context = attend(query_b, key_b, value_b, visible)
    pre_one = (
        x_in.astype(jnp.float32)
        + jnp.dot(context.astype(jnp.bfloat16), w_out, preferred_element_type=jnp.float32)
        + bias_o
    )
    normed1, inv_std1 = normalize(pre_one)
    hidden1 = normed1 * gain1 + shift1
    hidden1_b = hidden1.astype(jnp.bfloat16)
    up_pre = jnp.dot(hidden1_b, w_up, preferred_element_type=jnp.float32) + bias_up
    act_b = gelu_value(up_pre).astype(jnp.bfloat16)
    pre_two = hidden1 + jnp.dot(act_b, w_down, preferred_element_type=jnp.float32) + bias_down
    normed2, inv_std2 = normalize(pre_two)
    result = normed2 * gain2 + shift2
    kept_state = (
        x_in,
        query_b,
        key_b,
        value_b,
        log_total,
        context,
        normed1,
        inv_std1,
        hidden1_b,
        up_pre,
        act_b,
        normed2,
        inv_std2,
    )
    return (result, kept_state)


def empty_forward(x_in, visible, params):
    row_count = x_in.shape[0]
    zero_b = jnp.zeros((row_count, D), jnp.bfloat16)
    zero_f = jnp.zeros((row_count, D), jnp.float32)
    zero_col = jnp.zeros((row_count, 1), jnp.float32)
    kept_state = (
        zero_b,
        zero_b,
        zero_b,
        zero_b,
        jnp.zeros((HEADS, row_count, 1), jnp.float32),
        zero_f,
        zero_f,
        zero_col,
        zero_b,
        jnp.zeros((row_count, FF), jnp.float32),
        jnp.zeros((row_count, FF), jnp.bfloat16),
        zero_f,
        zero_col,
    )
    return (zero_f, kept_state)


def layer_backward(d_out, kept_state, visible, params):
    w_qkv, w_out, w_up, w_down, vec = params
    bias_q, bias_v, bias_o, gain1, shift1, bias_up, bias_down, gain2, shift2 = split_vector(vec)
    (
        x_in,
        query_b,
        key_b,
        value_b,
        log_total,
        context,
        normed1,
        inv_std1,
        hidden1_b,
        up_pre,
        act_b,
        normed2,
        inv_std2,
    ) = kept_state
    grad_gain2 = jnp.sum(d_out * normed2, axis=0)
    grad_shift2 = jnp.sum(d_out, axis=0)
    grad_pre2 = norm_back(d_out * gain2, normed2, inv_std2)
    grad_pre2_b = grad_pre2.astype(jnp.bfloat16)
    grad_bdown = jnp.sum(grad_pre2, axis=0)
    grad_up = right_dot(grad_pre2_b, w_down) * gelu_slope(up_pre)
    grad_up_b = grad_up.astype(jnp.bfloat16)
    grad_bup = jnp.sum(grad_up, axis=0)
    grad_h1 = grad_pre2 + right_dot(grad_up_b, w_up)
    grad_gain1 = jnp.sum(grad_h1 * normed1, axis=0)
    grad_shift1 = jnp.sum(grad_h1, axis=0)
    grad_pre1 = norm_back(grad_h1 * gain1, normed1, inv_std1)
    grad_pre1_b = grad_pre1.astype(jnp.bfloat16)
    grad_bout = jnp.sum(grad_pre1, axis=0)
    context_b = context.astype(jnp.bfloat16)
    grad_ctx_b = right_dot(grad_pre1_b, w_out).astype(jnp.bfloat16)
    grad_proj = attend_back(grad_ctx_b, query_b, key_b, value_b, log_total, context, visible)
    grad_proj_b = grad_proj.astype(jnp.bfloat16)
    grad_bq = jnp.sum(grad_proj[:, :D], axis=0)
    grad_bv = jnp.sum(grad_proj[:, 2 * D :], axis=0)
    grad_x = grad_pre1 + right_dot(grad_proj_b, w_qkv)
    grad_vec = jnp.concatenate(
        [
            grad_bq,
            grad_bv,
            grad_bout,
            grad_gain1,
            grad_shift1,
            grad_bup,
            grad_bdown,
            grad_gain2,
            grad_shift2,
        ]
    )
    operands = (x_in, grad_proj_b, context_b, grad_pre1_b, hidden1_b, grad_up_b, act_b, grad_pre2_b)
    return (grad_x, grad_vec, operands)


def empty_backward(d_out, kept_state, visible, params):
    row_count = d_out.shape[0]
    zero_d = jnp.zeros((row_count, D), jnp.bfloat16)
    zero_ff = jnp.zeros((row_count, FF), jnp.bfloat16)
    operands = (
        zero_d,
        jnp.zeros((row_count, 3 * D), jnp.bfloat16),
        zero_d,
        zero_d,
        zero_d,
        zero_ff,
        zero_ff,
        zero_d,
    )
    return (jnp.zeros_like(d_out), jnp.zeros(params[4].shape, jnp.float32), operands)


def weight_terms(operands, grad_vec):
    x_in, grad_proj_b, context_b, grad_pre1_b, hidden1_b, grad_up_b, act_b, grad_pre2_b = operands
    return (
        left_dot(x_in, grad_proj_b),
        left_dot(context_b, grad_pre1_b),
        left_dot(hidden1_b, grad_up_b),
        left_dot(act_b, grad_pre2_b),
        grad_vec,
    )


def body(ends, lengths, w_qkv, w_out, w_up, w_down, vectors):
    section_index = lax.axis_index("section")
    is_first = section_index == 0
    not_first = jnp.logical_not(is_first)
    local_rows = ends[0, :, 0]
    seq_lengths = lengths[:, 0]
    micro = local_rows.shape[0]
    row_count = local_rows.shape[1]
    shards = (w_qkv[0], w_out[0], w_up[0], w_down[0], vectors[0])
    params = (
        lax.all_gather(shards[0], "fsdp", axis=0, tiled=True),
        lax.all_gather(shards[1], "fsdp", axis=0, tiled=True),
        lax.all_gather(shards[2], "fsdp", axis=0, tiled=True),
        lax.all_gather(shards[3], "fsdp", axis=0, tiled=True),
        lax.all_gather(shards[4], "fsdp", axis=0, tiled=True),
    )
    positions = jnp.arange(row_count, dtype=jnp.int32)
    received = jnp.zeros((row_count, D), jnp.bfloat16)
    kept_steps = []
    outputs = []
    for tick in range(micro + 1):
        index_first = min(tick, micro - 1)
        index_second = max(tick - 1, 0)
        x_in = jnp.where(is_first, local_rows[index_first], received)
        length = jnp.where(is_first, seq_lengths[index_first], seq_lengths[index_second])
        visible = positions < length
        active = jnp.logical_or(
            jnp.logical_and(is_first, tick < micro), jnp.logical_and(not_first, tick >= 1)
        )
        result, kept_state = lax.cond(active, layer_forward, empty_forward, x_in, visible, params)
        kept_steps.append((kept_state, visible))
        outputs.append(result)
        if tick < micro:
            received = shifted(result.astype(jnp.bfloat16), "section", 1)
    params_back = (
        lax.all_gather(shards[0], "fsdp", axis=0, tiled=True),
        lax.all_gather(shards[1], "fsdp", axis=0, tiled=True),
        lax.all_gather(shards[2], "fsdp", axis=0, tiled=True),
        lax.all_gather(shards[3], "fsdp", axis=0, tiled=True),
        lax.all_gather(shards[4], "fsdp", axis=0, tiled=True),
    )
    shard_totals = tuple((jnp.zeros(shard.shape, jnp.float32) for shard in shards))
    vec_total = jnp.zeros(params_back[4].shape, jnp.float32)
    back_received = jnp.zeros((row_count, D), jnp.bfloat16)
    grad_steps = []
    operand_steps = []
    for tick in range(micro + 1):
        kept_state, visible = kept_steps[micro - tick]
        index_second = max(micro - 1 - tick, 0)
        cotangent = local_rows[index_second].astype(jnp.float32) * visible[:, None].astype(
            jnp.float32
        )
        d_out = jnp.where(is_first, back_received.astype(jnp.float32), cotangent)
        active = jnp.logical_or(
            jnp.logical_and(is_first, tick >= 1), jnp.logical_and(not_first, tick < micro)
        )
        grad_x, grad_vec, operands = lax.cond(
            active, layer_backward, empty_backward, d_out, kept_state, visible, params_back
        )
        grad_steps.append(grad_x)
        operand_steps.append(operands)
        vec_total = vec_total + grad_vec
        if tick < micro:
            back_received = shifted(grad_x.astype(jnp.bfloat16), "section", -1)
    chosen = []
    for batch_index in range(micro):
        chosen.append(
            jax.tree.map(
                lambda later, earlier: jnp.where(is_first, later, earlier),
                operand_steps[batch_index + 1],
                operand_steps[batch_index],
            )
        )
    joined = tuple((jnp.concatenate([item[slot] for item in chosen], axis=0) for slot in range(8)))
    shard_totals = lax.psum_scatter(
        weight_terms(joined, vec_total), "fsdp", scatter_dimension=0, tiled=True
    )
    values = []
    for batch_index in range(micro):
        values.append(
            jnp.where(is_first, grad_steps[micro - batch_index], outputs[batch_index + 1])
        )
    ends_out = jnp.stack(values)[None, :, None]
    return (
        ends_out,
        shard_totals[0][None],
        shard_totals[1][None],
        shard_totals[2][None],
        shard_totals[3][None],
        shard_totals[4][None],
    )


def solution(mesh):
    in_specs = (
        P("section", None, "fsdp", None, None),
        P(None, "fsdp"),
        P("section", "fsdp", None),
        P("section", "fsdp", None),
        P("section", "fsdp", None),
        P("section", "fsdp", None),
        P("section", "fsdp"),
    )
    out_specs = (
        P("section", None, "fsdp", None, None),
        P("section", "fsdp", None),
        P("section", "fsdp", None),
        P("section", "fsdp", None),
        P("section", "fsdp", None),
        P("section", "fsdp"),
    )
    return jax.shard_map(body, mesh=mesh, in_specs=in_specs, out_specs=out_specs, check_vma=False)
```

profile of v0, /device:TPU:0, one launch (start us, length us, event | category | flops | bytes accessed | tf_op | source)
XLA Modules:
  0.0 910.8 jit_solution(7794618358027764625)
XLA Ops:
  13.0 63.3 %all-reduce = bf16[9216]{0:T(1024)(128)(2,1)S(1)} all-reduce(bf16[9216]{0:T(1024)(128)(2,1)S(1)} %dynamic-update-slice), channel_id=3, replica_groups=mesh['section'=2,'fsdp'=16] {'fsdp'}, use_global_device_ids=true, to_apply=%add | all-reduce | flops 9216 | bytes 36864 | tf_op jit(solution)/shard_map/all_gather | solution.py:304
  78.4 2.4 fusion.113
  80.8 19.1 %all-gather.10.cloned.1.call-done = bf16[1,768,2304]{2,1,0:T(8,128)(2,1)} async-done(((bf16[1,48,2304]{2,1,0:T(8,128)(2,1)}), bf16[1,768,2304]{2,1,0:T(8,128)(2,1)}) %all-gather.10.cloned.1.call-update) | async-done | bytes 3538960 | tf_op jit(solution)/shard_map/all_gather | solution.py:275
  99.9 54.6 %all-gather.14.cloned.1.call-done = bf16[1,768,3072]{2,1,0:T(8,128)(2,1)} async-done(((bf16[1,48,3072]{2,1,0:T(8,128)(2,1)}), bf16[1,768,3072]{2,1,0:T(8,128)(2,1)}) %all-gather.14.cloned.1.call-update) | async-done | bytes 4718608 | tf_op jit(solution)/shard_map/all_gather | solution.py:277
  154.4 54.0 %all-gather.16.cloned.1.call-done = bf16[1,3072,768]{2,1,0:T(8,128)(2,1)} async-done(((bf16[1,192,768]{2,1,0:T(8,128)(2,1)}), bf16[1,3072,768]{2,1,0:T(8,128)(2,1)}) %all-gather.16.cloned.1.call-update) | async-done | bytes 4718608 | tf_op jit(solution)/shard_map/all_gather | solution.py:278
  208.4 30.2 %conditional.6 = (f32[256,768]{1,0:T(8,128)}, bf16[256,768]{1,0:T(8,128)(2,1)}, bf16[256,768]{1,0:T(8,128)(2,1)}, bf16[256,768]{1,0:T(8,128)(2,1)}, bf16[256,768...) conditional(s32[]{:T(128)} %convert_element_type.252, () %tuple.66, ...), branch_computations={%region_0.1_spmd, %region_1.8_spmd} | conditional | flops 3845256704 | bytes 99879160 | solution.py:294
  209.8 3.2 fusion.144
  218.8 2.9 fusion.1
  226.5 6.4 multiply_convert_fusion
  232.9 3.1 fusion.122
  242.8 7.7 collective-permute-done
  250.5 30.0 %conditional.7 = (f32[256,768]{1,0:T(8,128)S(1)}, bf16[256,768]{1,0:T(8,128)(2,1)S(1)}, bf16[256,768]{1,0:T(8,128)(2,1)}, bf16[256,768]{1,0:T(8,128)(2,1)}, bf16...) conditional(s32[]{:T(128)} %convert_element_type.255, () %tuple.69, ...), branch_computations={%region_8.9_spmd, %region_9.16_spmd} | conditional | flops 3845256704 | bytes 101771512 | solution.py:294
  252.2 3.2 fusion.145
  262.9 2.8 fusion.13
  269.3 6.4 multiply_convert_fusion.1
  275.7 3.1 fusion.125
  280.6 4.4 collective-permute-start.1
  287.4 5.8 collective-permute-done.1
  293.2 9.3 %conditional.8 = (f32[256,768]{1,0:T(8,128)}, bf16[256,768]{1,0:T(8,128)(2,1)}, bf16[256,768]{1,0:T(8,128)(2,1)S(1)}, bf16[256,768]{1,0:T(8,128)(2,1)S(1)}, bf16...) conditional(s32[]{:T(128)} %convert_element_type.258, () %tuple.72, ...), branch_computations={%region_16.17_spmd, %region_17.24_spmd} | conditional | flops 3845256704 | bytes 108112248 | solution.py:294
  302.5 9.4 %conditional.9 = (bf16[256,768]{1,0:T(8,128)(2,1)}, f32[9216]{0:T(1024)}, bf16[256,768]{1,0:T(8,128)(2,1)}, bf16[256,2304]{0,1:T(8,128)(2,1)}, bf16[256,768]{1,0...) conditional(s32[]{:T(128)} %convert_element_type.258, () %tuple.71, ...), branch_computations={%region_24.25_spmd, %region_25.40_spmd} | conditional | flops 4158836736 | bytes 114754600 | solution.py:321
  313.2 79.4 %collective-permute-done.2 = bf16[256,768]{1,0:T(8,128)(2,1)S(1)} collective-permute-done((bf16[256,768]{1,0:T(8,128)(2,1)}, bf16[256,768]{1,0:T(8,128)(2,1)S(1)}, u32[]{:S(2)}, u32[]{:S(2)}) %collective-permute-start.2) | collective-permute-done | bytes 393248 | tf_op jit(solution)/shard_map/ppermute | solution.py:15
  392.6 54.5 %conditional.10 = (f32[256,768]{1,0:T(8,128)}, f32[9216]{0:T(1024)}, bf16[256,768]{1,0:T(8,128)(2,1)}, bf16[256,2304]{0,1:T(8,128)(2,1)}, bf16[256,768]{1,0:T(8,...) conditional(s32[]{:T(128)} %convert_element_type.255, () %tuple.68, ...), branch_computations={%region_40.41_spmd, %region_41.56_spmd} | conditional | flops 4157853696 | bytes 142573584 | solution.py:321
  397.4 5.7 fusion.133
  403.1 3.9 multiply_reduce_fusion.13
  412.4 2.3 fusion.148
  415.9 2.9 multiply_convert_fusion.4
  422.7 4.0 fusion.134
  440.6 2.2 pad_maximum_fusion.1
  442.8 3.4 convolution_add_fusion.11
  447.2 2.6 fusion.141
  451.7 9.2 %collective-permute-done.3 = bf16[256,768]{1,0:T(8,128)(2,1)S(1)} collective-permute-done((bf16[256,768]{1,0:T(8,128)(2,1)S(1)}, bf16[256,768]{1,0:T(8,128)(2,1)S(1)}, u32[]{:S(2)}, u32[]{:S(2)}) %collective-permute-start.3) | collective-permute-done | bytes 393248 | tf_op jit(solution)/shard_map/ppermute | solution.py:15
  461.0 52.0 %conditional.11 = (f32[256,768]{1,0:T(8,128)}, f32[9216]{0:T(1024)}, bf16[256,768]{1,0:T(8,128)(2,1)}, bf16[256,2304]{0,1:T(8,128)(2,1)}, bf16[256,768]{1,0:T(8,...) conditional(s32[]{:T(128)} %convert_element_type.252, () %tuple.65, ...), branch_computations={%region_56.57_spmd, %region_57.72_spmd} | conditional | flops 4157853696 | bytes 134708144 | solution.py:321
  464.6 5.6 fusion.137
  470.2 3.9 multiply_reduce_fusion.20
  479.4 2.3 fusion.149
  481.8 2.9 multiply_convert_fusion.5
  488.6 4.0 fusion.138
  506.5 2.2 pad_maximum_fusion.2
  508.7 3.4 convolution_add_fusion.13
  519.9 5.0 fusion.89
  525.0 2.3 broadcast_select_fusion.10
  527.2 3.5 broadcast_select_fusion.4
  530.8 5.1 fusion.85
  536.0 6.2 fusion.81
  543.8 58.0 %all-reduce.1 = f32[9216]{0:T(1024)S(1)} all-reduce(f32[9216]{0:T(1024)S(1)} %add_add_fusion), channel_id=11, replica_groups=mesh['section'=2,'fsdp'=16] {'fsdp'}, use_global_device_ids=true, to_apply=%region_76.77.clone | all-reduce | flops 9216 | bytes 73728
  605.0 66.9 %reduce-scatter.5.cloned.1.call-done = f32[48,2304]{1,0:T(8,128)} async-done(((f32[768,2304]{1,0:T(8,128)}), f32[48,2304]{1,0:T(8,128)}) %reduce-scatter.5.cloned.1.call-update) | async-done | bytes 442384 | tf_op jit(solution)/shard_map/reduce_scatter | solution.py:339
  671.9 115.5 %reduce-scatter.11.cloned.1.call-done = f32[192,768]{1,0:T(8,128)} async-done(((f32[3072,768]{1,0:T(8,128)}), f32[192,768]{1,0:T(8,128)}) %reduce-scatter.11.cloned.1.call-update) | async-done | bytes 589840 | tf_op jit(solution)/shard_map/reduce_scatter | solution.py:339
  787.5 116.4 %reduce-scatter.9.cloned.1.call-done = f32[48,3072]{1,0:T(8,128)} async-done(((f32[768,3072]{1,0:T(8,128)}), f32[48,3072]{1,0:T(8,128)}) %reduce-scatter.9.cloned.1.call-update) | async-done | bytes 589840 | tf_op jit(solution)/shard_map/reduce_scatter | solution.py:339
  (317 shorter events, 130.0 us)
Async XLA Ops:
  7.2 73.6 %all-gather.12.cloned.1.call-start = ((), (), s32[]{:S(2)}) async-start(), calls=%async_computation.9 | async-start | bytes 1253376 | tf_op jit(solution)/shard_map/all_gather | solution.py:276
  7.9 92.0 %all-gather.10.cloned.1.call-start = ((), (), s32[]{:S(2)}) async-start(), calls=%async_computation.8 | async-start | bytes 3760128 | tf_op jit(solution)/shard_map/all_gather | solution.py:275
  8.6 145.8 %all-gather.14.cloned.1.call-start = ((), (), s32[]{:S(2)}) async-start(), calls=%async_computation.10 | async-start | bytes 5013504 | tf_op jit(solution)/shard_map/all_gather | solution.py:277
  9.4 199.0 %all-gather.16.cloned.1.call-start = ((), (), s32[]{:S(2)}) async-start(), calls=%async_computation.11 | async-start | bytes 5013504 | tf_op jit(solution)/shard_map/all_gather | solution.py:278
  10.0 595.0 %reduce-scatter.7.cloned.1.call-start = ((), (), s32[]{:S(2)}) async-start(), calls=%async_computation.5 | async-start | bytes 2506752 | tf_op jit(solution)/shard_map/reduce_scatter | solution.py:339
  76.3 132.0 %copy-start.66 = (bf16[9216]{0:T(1024)(128)(2,1)}, bf16[9216]{0:T(1024)(128)(2,1)S(1)}, u32[]{:S(2)}) copy-start(bf16[9216]{0:T(1024)(128)(2,1)S(1)} %all-reduce) | copy-start | bytes 55300
  78.4 130.0 %copy-start.83 = (pred[256]{0:T(512)(128)(4,1)}, pred[256]{0:T(512)(128)(4,1)S(1)}, u32[]{:S(2)}) copy-start(pred[256]{0:T(512)(128)(4,1)S(1)} %iota_compare_fusion.2) | copy-start | bytes 772
  208.4 8.6 copy-start.85
  221.6 11.3 %copy-start.12 = (f32[12,64,256]{2,1,0:T(8,128)}, f32[12,64,256]{2,1,0:T(8,128)S(1)}, u32[]{:S(2)}) copy-start(f32[12,64,256]{2,1,0:T(8,128)S(1)} %fusion.1) | copy-start | bytes 2359300 | tf_op jit(solution)/shard_map/cond
  224.4 8.5 slice-start.6
  226.5 6.4 copy-start.80
  226.5 6.4 slice-start.7
  238.6 11.8 %copy-start.28 = (f32[256,768]{1,0:T(8,128)}, f32[256,768]{1,0:T(8,128)S(1)}, u32[]{:S(2)}) copy-start(f32[256,768]{1,0:T(8,128)S(1)} %get-tuple-element.478) | copy-start | bytes 2359300
  240.1 10.4 %collective-permute-start = (bf16[256,768]{1,0:T(8,128)(2,1)S(1)}, bf16[256,768]{1,0:T(8,128)(2,1)S(1)}, u32[]{:S(2)}, u32[]{:S(2)}) collective-permute-start(bf16[256,768]{1,0:T(8,128)(2,1)S(1)} %convert_element_type.256), channel_id=1, source_target_pairs={{0,16},{1,17},{2,18},{3,19},{4,20},{5,21},{6,22},{7,23},{8,24},{9,... | collective-permute-start | bytes 1179656 | tf_op jit(solution)/shard_map/ppermute | solution.py:15
  242.8 7.7 copy-start.86
  250.7 9.3 %copy-start.87 = (pred[256]{0:T(512)(128)(4,1)}, pred[256]{0:T(512)(128)(4,1)S(1)}, u32[]{:S(2)}) copy-start(pred[256]{0:T(512)(128)(4,1)S(1)} %get-tuple-element.287) | copy-start | bytes 772 | tf_op jit(solution)/shard_map/cond
  252.2 13.5 %copy-start.36 = (bf16[256,768]{1,0:T(8,128)(2,1)}, bf16[256,768]{1,0:T(8,128)(2,1)S(1)}, u32[]{:S(2)}) copy-start(bf16[256,768]{1,0:T(8,128)(2,1)S(1)} %broadcast_select_fusion.1) | copy-start | bytes 1179652 | tf_op jit(solution)/shard_map/cond
  265.7 10.0 %copy-start.16 = (f32[12,64,256]{2,1,0:T(8,128)}, f32[12,64,256]{2,1,0:T(8,128)S(1)}, u32[]{:S(2)}) copy-start(f32[12,64,256]{2,1,0:T(8,128)S(1)} %fusion.13) | copy-start | bytes 2359300 | tf_op jit(solution)/shard_map/cond
  267.2 8.5 slice-start.8
  269.3 6.4 copy-start.81
  269.3 6.4 slice-start.9
  280.5 12.8 %copy-start.26 = (f32[256,768]{1,0:T(8,128)}, f32[256,768]{1,0:T(8,128)S(1)}, u32[]{:S(2)}) copy-start(f32[256,768]{1,0:T(8,128)S(1)} %get-tuple-element.451) | copy-start | bytes 2359300
  280.5 12.8 %copy-start.30 = (f32[256,768]{1,0:T(8,128)}, f32[256,768]{1,0:T(8,128)S(1)}, u32[]{:S(2)}) copy-start(f32[256,768]{1,0:T(8,128)S(1)} %get-tuple-element.466) | copy-start | bytes 2359300
  280.5 12.7 %copy-start.38 = (bf16[256,768]{1,0:T(8,128)(2,1)}, bf16[256,768]{1,0:T(8,128)(2,1)S(1)}, u32[]{:S(2)}) copy-start(bf16[256,768]{1,0:T(8,128)(2,1)S(1)} %get-tuple-element.474) | copy-start | bytes 1179652
  280.6 12.7 %collective-permute-start.1 = (bf16[256,768]{1,0:T(8,128)(2,1)S(1)}, bf16[256,768]{1,0:T(8,128)(2,1)S(1)}, u32[]{:S(2)}, u32[]{:S(2)}) collective-permute-start(bf16[256,768]{1,0:T(8,128)(2,1)S(1)} %convert_element_type.259), channel_id=1, source_target_pairs={{0,16},{1,17},{2,18},{3,19},{4,20},{5,21},{6,22},{7,23},{8,24},{9,... | collective-permute-start | bytes 1179656 | tf_op jit(solution)/shard_map/ppermute | solution.py:15
  311.9 80.7 %collective-permute-start.2 = (bf16[256,768]{1,0:T(8,128)(2,1)}, bf16[256,768]{1,0:T(8,128)(2,1)S(1)}, u32[]{:S(2)}, u32[]{:S(2)}) collective-permute-start(bf16[256,768]{1,0:T(8,128)(2,1)} %get-tuple-element.465), channel_id=1, source_target_pairs={{16,0},{17,1},{18,2},{19,3},{20,4},{21,5},{22,6},{23,7},{24,8},{25... | collective-permute-start | bytes 1179656 | tf_op jit(solution)/shard_map/ppermute | solution.py:15
  396.6 6.5 slice-start.2
  397.4 5.7 slice-start.3
  412.2 6.6 copy-start.57
  426.7 16.1 %copy-start.7 = (bf16[768,2304]{1,0:T(8,128)(2,1)S(1)}, bf16[768,2304]{1,0:T(8,128)(2,1)}, u32[]{:S(2)}) copy-start(bf16[768,2304]{1,0:T(8,128)(2,1)} %get-tuple-element.341) | copy-start | bytes 10616836 | tf_op jit(solution)/shard_map/cond
  428.2 14.6 %copy-start.62 = (f32[256,768]{1,0:T(8,128)S(1)}, f32[256,768]{1,0:T(8,128)}, u32[]{:S(2)}) copy-start(f32[256,768]{1,0:T(8,128)} %copy-done.61) | copy-start | bytes 2359300 | tf_op jit(solution)/shard_map/cond
  447.2 13.8 %copy-start = (bf16[1,768,768]{2,1,0:T(8,128)(2,1)S(1)}, bf16[1,768,768]{2,1,0:T(8,128)(2,1)}, u32[]{:S(2)}) copy-start(bf16[1,768,768]{2,1,0:T(8,128)(2,1)} %all-gather.12.cloned.1.call-done) | copy-start | bytes 3538948
  447.2 13.8 %copy-start.13 = (f32[256,768]{0,1:T(8,128)S(1)}, f32[256,768]{0,1:T(8,128)}, u32[]{:S(2)}) copy-start(f32[256,768]{0,1:T(8,128)} %get-tuple-element.485) | copy-start | bytes 2359300
  447.2 13.8 %copy-start.29 = (f32[256,768]{1,0:T(8,128)S(1)}, f32[256,768]{1,0:T(8,128)}, u32[]{:S(2)}) copy-start(f32[256,768]{1,0:T(8,128)} %copy-done.28) | copy-start | bytes 2359300
  447.2 13.8 %copy-start.32 = (f32[256,768]{1,0:T(8,128)S(1)}, f32[256,768]{1,0:T(8,128)}, u32[]{:S(2)}) copy-start(f32[256,768]{1,0:T(8,128)} %get-tuple-element.1065) | copy-start | bytes 2359300
  447.2 13.8 %copy-start.41 = (bf16[256,768]{1,0:T(8,128)(2,1)S(1)}, bf16[256,768]{1,0:T(8,128)(2,1)}, u32[]{:S(2)}) copy-start(bf16[256,768]{1,0:T(8,128)(2,1)} %get-tuple-element.481) | copy-start | bytes 1179652
  447.2 13.8 %copy-start.84 = (pred[256]{0:T(512)(128)(4,1)S(1)}, pred[256]{0:T(512)(128)(4,1)}, u32[]{:S(2)}) copy-start(pred[256]{0:T(512)(128)(4,1)} %copy-done.83) | copy-start | bytes 772
  449.8 11.1 %collective-permute-start.3 = (bf16[256,768]{1,0:T(8,128)(2,1)S(1)}, bf16[256,768]{1,0:T(8,128)(2,1)S(1)}, u32[]{:S(2)}, u32[]{:S(2)}) collective-permute-start(bf16[256,768]{1,0:T(8,128)(2,1)S(1)} %get-tuple-element.1063), channel_id=1, source_target_pairs={{16,0},{17,1},{18,2},{19,3},{20,4},{21,5},{22,6},{23,7},{24,8},{25... | collective-permute-start | bytes 1179656 | tf_op jit(solution)/shard_map/ppermute | solution.py:15
  461.4 17.4 %copy-start.14 = (f32[256,768]{0,1:T(8,128)}, f32[256,768]{0,1:T(8,128)S(1)}, u32[]{:S(2)}) copy-start(f32[256,768]{0,1:T(8,128)S(1)} %get-tuple-element.363) | copy-start | bytes 2359300 | tf_op jit(solution)/shard_map/cond
  463.8 6.4 slice-start.4
  464.6 5.6 slice-start.5
  492.6 16.1 %copy-start.8 = (bf16[768,2304]{1,0:T(8,128)(2,1)S(1)}, bf16[768,2304]{1,0:T(8,128)(2,1)}, u32[]{:S(2)}) copy-start(bf16[768,2304]{1,0:T(8,128)(2,1)} %get-tuple-element.364) | copy-start | bytes 10616836 | tf_op jit(solution)/shard_map/cond
  494.1 14.6 %copy-start.64 = (f32[256,768]{1,0:T(8,128)S(1)}, f32[256,768]{1,0:T(8,128)}, u32[]{:S(2)}) copy-start(f32[256,768]{1,0:T(8,128)} %copy-done.63) | copy-start | bytes 2359300 | tf_op jit(solution)/shard_map/cond
  516.8 155.1 %reduce-scatter.5.cloned.1.call-start = ((), (), s32[]{:S(2)}) async-start(), calls=%async_computation.4 | async-start | bytes 7520256 | tf_op jit(solution)/shard_map/reduce_scatter | solution.py:339
  524.9 262.5 %reduce-scatter.11.cloned.1.call-start = ((), (), s32[]{:S(2)}) async-start(), calls=%async_computation.7 | async-start | bytes 10027008 | tf_op jit(solution)/shard_map/reduce_scatter | solution.py:339
  535.9 367.9 %reduce-scatter.9.cloned.1.call-start = ((), (), s32[]{:S(2)}) async-start(), calls=%async_computation.6 | async-start | bytes 10027008 | tf_op jit(solution)/shard_map/reduce_scatter | solution.py:339
  542.2 60.3 %copy-start.27 = (f32[256,768]{1,0:T(8,128)S(1)}, f32[256,768]{1,0:T(8,128)}, u32[]{:S(2)}) copy-start(f32[256,768]{1,0:T(8,128)} %copy-done.26) | copy-start | bytes 2359300
  542.2 61.5 %copy-start.65 = (f32[1,256,768]{2,1,0:T(8,128)S(1)}, f32[1,256,768]{2,1,0:T(8,128)}, u32[]{:S(2)}) copy-start(f32[1,256,768]{2,1,0:T(8,128)} %get-tuple-element.1064) | copy-start | bytes 2359300
  (35 other events, 100.8 us)
Sparse Core Ops, SparseCore 0:
  10.3 41.1 all-gather.11
  53.7 46.0 all-gather.9
  102.2 52.2 all-gather.13
  156.6 51.7 all-gather.15
  516.9 60.9 reduce-scatter.6
  582.9 88.9 reduce-scatter.4
  676.6 110.8 reduce-scatter.10
  792.7 111.0 reduce-scatter.8
where the time goes:
time: 921 us; the launch traced here: 911 us
  waiting for transfers between devices  531 us (58%)
  blocking collectives  121 us (13%)
  matrix products  107 us (12%)
  local copies, waits for them, and re-layouts  67.7 us (7%)
  other arithmetic  54.7 us (6%)
  between operations  17.4 us (2%)
    reduce_scatter x4, waiting for transfers between devices, body(): lax.psum_scatter(weight_terms(joined, vec_total), 'fsdp', scatter_dimensi...  299 us
    ppermute x4, waiting for transfers between devices, shifted(): lax.ppermute(value, axis, [(source, source + steps) for source in range(f...  102 us
    all_gather x1, blocking collectives, body(): lax.all_gather(shards[4], 'fsdp', axis=0, tiled=True)  63.3 us
    unnamed x1, blocking collectives  58 us
    all_gather x1, waiting for transfers between devices, body(): lax.all_gather(shards[2], 'fsdp', axis=0, tiled=True)  54.6 us
    all_gather x1, waiting for transfers between devices, body(): lax.all_gather(shards[3], 'fsdp', axis=0, tiled=True)  54 us
    dot_general x8, matrix products, right_dot(): lax.dot_general(left, right, (((1,), (1,)), ((), ())), preferred_element_...  28.8 us
    cond x126, local copies, waits for them, and re-layouts  28 us
  transfers between devices with their start and end apart: 12, of which 10 were waited for; matrix products, arithmetic and copies ran while one was open for 4% of the time, Pallas kernels for 0%

commit v1 on v0

v1 whole, which is shorter than its diff:
```python
import jax
import jax.numpy as jnp
from jax import lax
from jax.sharding import PartitionSpec as P

D = 768
HEADS = 12
FF = 3072
HEAD = 64


def shifted(value, axis, steps):
    count = lax.axis_size(axis)
    first, last = (max(0, -steps), min(count, count - steps))
    return lax.ppermute(value, axis, [(source, source + steps) for source in range(first, last)])


def split_vector(vec):
    flat_vec = vec.astype(jnp.float32)
    widths = [D, D, D, D, D, FF, D, D, D]
    pieces = []
    offset = 0
    for width in widths:
        pieces.append(flat_vec[offset : offset + width])
        offset = offset + width
    return tuple(pieces)


def normalize(hidden):
    mean_row = jnp.mean(hidden, axis=-1, keepdims=True)
    centred = hidden - mean_row
    variance = jnp.mean(centred * centred, axis=-1, keepdims=True)
    inv_std = lax.rsqrt(variance + 1e-12)
    return (centred * inv_std, inv_std)


def norm_back(grad_n, normed, inv_std):
    return inv_std * (
        grad_n
        - jnp.mean(grad_n, axis=-1, keepdims=True)
        - normed * jnp.mean(grad_n * normed, axis=-1, keepdims=True)
    )


def gelu_value(up_in):
    return 0.5 * up_in * (1.0 + lax.erf(up_in * 0.7071067811865476))


def gelu_slope(up_in):
    return (
        0.5 * (1.0 + lax.erf(up_in * 0.7071067811865476))
        + up_in * jnp.exp(-0.5 * up_in * up_in) * 0.3989422804014327
    )


def left_dot(left, right):
    return lax.dot_general(
        left, right, (((0,), (0,)), ((), ())), preferred_element_type=jnp.float32
    )


def right_dot(left, right):
    return lax.dot_general(
        left, right, (((1,), (1,)), ((), ())), preferred_element_type=jnp.float32
    )


def rows_of(value, groups):
    return value.reshape(groups, value.shape[0] // groups, HEADS, HEAD)


def scores_of(query_b, key_b, visible):
    groups = visible.shape[0]
    scores = jnp.einsum(
        "bqhd,bkhd->bhqk",
        rows_of(query_b, groups),
        rows_of(key_b, groups),
        preferred_element_type=jnp.float32,
    ) * HEAD ** (-0.5)
    return jnp.where(visible[:, None, None, :], scores, -1e30)


def attend(query_b, key_b, value_b, visible):
    groups = visible.shape[0]
    masked = scores_of(query_b, key_b, visible)
    row_peak = jnp.max(masked, axis=-1, keepdims=True)
    log_total = row_peak + jnp.log(jnp.sum(jnp.exp(masked - row_peak), axis=-1, keepdims=True))
    probs_b = jnp.exp(masked - log_total).astype(jnp.bfloat16)
    context = jnp.einsum(
        "bhqk,bkhd->bqhd", probs_b, rows_of(value_b, groups), preferred_element_type=jnp.float32
    )
    return (log_total, context.reshape(-1, D))


def attend_back(grad_ctx_b, query_b, key_b, value_b, log_total, context, visible):
    groups = visible.shape[0]
    masked = scores_of(query_b, key_b, visible)
    attn_probs = jnp.exp(masked - log_total)
    probs_b = attn_probs.astype(jnp.bfloat16)
    grad_heads = rows_of(grad_ctx_b, groups)
    grad_v = jnp.einsum("bhqk,bqhd->bkhd", probs_b, grad_heads, preferred_element_type=jnp.float32)
    grad_p = jnp.einsum(
        "bqhd,bkhd->bhqk", grad_heads, rows_of(value_b, groups), preferred_element_type=jnp.float32
    )
    delta_rows = jnp.sum(grad_heads.astype(jnp.float32) * rows_of(context, groups), axis=-1)
    grad_s = attn_probs * (grad_p - jnp.swapaxes(delta_rows, 1, 2)[..., None]) * HEAD ** (-0.5)
    grad_s_b = grad_s.astype(jnp.bfloat16)
    grad_q = jnp.einsum(
        "bhqk,bkhd->bqhd", grad_s_b, rows_of(key_b, groups), preferred_element_type=jnp.float32
    )
    grad_k = jnp.einsum(
        "bhqk,bqhd->bkhd", grad_s_b, rows_of(query_b, groups), preferred_element_type=jnp.float32
    )
    return jnp.concatenate(
        [grad_q.reshape(-1, D), grad_k.reshape(-1, D), grad_v.reshape(-1, D)], axis=1
    )


def layer_forward(x_in, visible, params):
    w_qkv, w_out, w_up, w_down, vec = params
    bias_q, bias_v, bias_o, gain1, shift1, bias_up, bias_down, gain2, shift2 = split_vector(vec)
    projected = jnp.dot(x_in, w_qkv, preferred_element_type=jnp.float32)
    query_b = (projected[:, :D] + bias_q).astype(jnp.bfloat16)
    key_b = projected[:, D : 2 * D].astype(jnp.bfloat16)
    value_b = (projected[:, 2 * D :] + bias_v).astype(jnp.bfloat16)
    log_total, context = attend(query_b, key_b, value_b, visible)
    pre_one = (
        x_in.astype(jnp.float32)
        + jnp.dot(context.astype(jnp.bfloat16), w_out, preferred_element_type=jnp.float32)
        + bias_o
    )
    normed1, inv_std1 = normalize(pre_one)
    hidden1 = normed1 * gain1 + shift1
    hidden1_b = hidden1.astype(jnp.bfloat16)
    up_pre = jnp.dot(hidden1_b, w_up, preferred_element_type=jnp.float32) + bias_up
    act_b = gelu_value(up_pre).astype(jnp.bfloat16)
    pre_two = hidden1 + jnp.dot(act_b, w_down, preferred_element_type=jnp.float32) + bias_down
    normed2, inv_std2 = normalize(pre_two)
    result = normed2 * gain2 + shift2
    kept_state = (
        x_in,
        query_b,
        key_b,
        value_b,
        log_total,
        context,
        normed1,
        inv_std1,
        hidden1_b,
        up_pre,
        act_b,
        normed2,
        inv_std2,
    )
    return (result, kept_state)


def layer_backward(d_out, kept_state, visible, params):
    w_qkv, w_out, w_up, w_down, vec = params
    bias_q, bias_v, bias_o, gain1, shift1, bias_up, bias_down, gain2, shift2 = split_vector(vec)
    (
        x_in,
        query_b,
        key_b,
        value_b,
        log_total,
        context,
        normed1,
        inv_std1,
        hidden1_b,
        up_pre,
        act_b,
        normed2,
        inv_std2,
    ) = kept_state
    grad_gain2 = jnp.sum(d_out * normed2, axis=0)
    grad_shift2 = jnp.sum(d_out, axis=0)
    grad_pre2 = norm_back(d_out * gain2, normed2, inv_std2)
    grad_pre2_b = grad_pre2.astype(jnp.bfloat16)
    grad_bdown = jnp.sum(grad_pre2, axis=0)
    grad_up = right_dot(grad_pre2_b, w_down) * gelu_slope(up_pre)
    grad_up_b = grad_up.astype(jnp.bfloat16)
    grad_bup = jnp.sum(grad_up, axis=0)
    grad_h1 = grad_pre2 + right_dot(grad_up_b, w_up)
    grad_gain1 = jnp.sum(grad_h1 * normed1, axis=0)
    grad_shift1 = jnp.sum(grad_h1, axis=0)
    grad_pre1 = norm_back(grad_h1 * gain1, normed1, inv_std1)
    grad_pre1_b = grad_pre1.astype(jnp.bfloat16)
    grad_bout = jnp.sum(grad_pre1, axis=0)
    context_b = context.astype(jnp.bfloat16)
    grad_ctx_b = right_dot(grad_pre1_b, w_out).astype(jnp.bfloat16)
    grad_proj = attend_back(grad_ctx_b, query_b, key_b, value_b, log_total, context, visible)
    grad_proj_b = grad_proj.astype(jnp.bfloat16)
    grad_bq = jnp.sum(grad_proj[:, :D], axis=0)
    grad_bv = jnp.sum(grad_proj[:, 2 * D :], axis=0)
    grad_x = grad_pre1 + right_dot(grad_proj_b, w_qkv)
    grad_vec = jnp.concatenate(
        [
            grad_bq,
            grad_bv,
            grad_bout,
            grad_gain1,
            grad_shift1,
            grad_bup,
            grad_bdown,
            grad_gain2,
            grad_shift2,
        ]
    )
    operands = (
        (x_in, grad_proj_b),
        (context_b, grad_pre1_b),
        (hidden1_b, grad_up_b),
        (act_b, grad_pre2_b),
    )
    return (grad_x, grad_vec, operands)


def gather_params(shards):
    return tuple(lax.all_gather(shard, "fsdp", axis=0, tiled=True) for shard in shards)


def gather_with_vector(w_shard, vec_shard):
    count = lax.axis_size("fsdp")
    rows, width = w_shard.shape
    padded = jnp.pad(vec_shard[None, :], ((0, 15), (0, width - vec_shard.shape[0])))
    joined = lax.all_gather(jnp.concatenate([w_shard, padded], axis=0), "fsdp", axis=0)
    weight = joined[:, :rows].reshape(count * rows, width)
    return weight, joined[:, rows, : vec_shard.shape[0]].reshape(-1)


def scatter_sum(value):
    total = lax.psum_scatter(
        value.astype(jnp.bfloat16), "fsdp", scatter_dimension=0, tiled=True
    )
    return total.astype(jnp.float32)


def scatter_with_vector(w_grad, vec_grad):
    count = lax.axis_size("fsdp")
    width = w_grad.shape[1]
    rows = w_grad.shape[0] // count
    share = vec_grad.shape[0] // count
    padded = jnp.pad(vec_grad.reshape(count, 1, share), ((0, 0), (0, 15), (0, width - share)))
    joined = jnp.concatenate([w_grad.reshape(count, rows, width), padded], axis=1)
    total = scatter_sum(joined.reshape(-1, width))
    return total[:rows], total[rows, :share]


def body(ends, lengths, w_qkv, w_out, w_up, w_down, vectors):
    is_first = lax.axis_index("section") == 0
    micro, row_count = ends.shape[1], ends.shape[3]
    local_rows = ends[0, :, 0].reshape(micro * row_count, D)
    positions = jnp.arange(row_count, dtype=jnp.int32)
    visible = positions[None, :] < lengths[:, 0][:, None]
    full_out, full_vec = gather_with_vector(w_out[0], vectors[0])
    full_qkv, full_up, full_down = gather_params((w_qkv[0], w_up[0], w_down[0]))
    params = (full_qkv, full_out, full_up, full_down, full_vec)
    early, _ = layer_forward(local_rows, visible, params)
    received = shifted(early.astype(jnp.bfloat16), "section", 1)
    x_in = jnp.where(is_first, local_rows, received)
    result, kept_state = layer_forward(x_in, visible, params)
    row_mask = visible.reshape(-1, 1).astype(jnp.float32)
    cotangent = local_rows.astype(jnp.float32) * row_mask
    early_grad, _, _ = layer_backward(cotangent, kept_state, visible, params)
    back_received = shifted(early_grad.astype(jnp.bfloat16), "section", -1)
    d_out = jnp.where(is_first, back_received.astype(jnp.float32), cotangent)
    grad_x, grad_vec, operands = layer_backward(d_out, kept_state, visible, params)
    grad_down = scatter_sum(left_dot(*operands[3]))
    grad_up = scatter_sum(left_dot(*operands[2]))
    grad_qkv = scatter_sum(left_dot(*operands[0]))
    grad_out, grad_vectors = scatter_with_vector(left_dot(*operands[1]), grad_vec)
    ends_out = jnp.where(is_first, grad_x, result).reshape(1, micro, 1, row_count, D)
    return (
        ends_out,
        grad_qkv[None],
        grad_out[None],
        grad_up[None],
        grad_down[None],
        grad_vectors[None],
    )


def solution(mesh):
    in_specs = (
        P("section", None, "fsdp", None, None),
        P(None, "fsdp"),
        P("section", "fsdp", None),
        P("section", "fsdp", None),
        P("section", "fsdp", None),
        P("section", "fsdp", None),
        P("section", "fsdp"),
    )
    out_specs = (
        P("section", None, "fsdp", None, None),
        P("section", "fsdp", None),
        P("section", "fsdp", None),
        P("section", "fsdp", None),
        P("section", "fsdp", None),
        P("section", "fsdp"),
    )
    return jax.shard_map(body, mesh=mesh, in_specs=in_specs, out_specs=out_specs, check_vma=False)
```

time: 921 us -> 669 us (0.73)
  blocking collectives: 121 us -> 0 us
  waiting for transfers between devices: 531 us -> 449 us
  other arithmetic: 54.7 us -> 29.7 us
    ppermute x4 -> x2, waiting for transfers between devices: 102 us -> 36.6 us  [shifted(): lax.ppermute(value, axis, [(source, source + steps) for source in range(f...]
    all_gather x1 -> x0, blocking collectives: 63.3 us -> none  [body(): lax.all_gather(shards[4], 'fsdp', axis=0, tiled=True)]
    unnamed x1 -> x0, blocking collectives: 58 us -> none
    reduce_scatter x4, waiting for transfers between devices: 299 us -> 244 us  [scatter_sum(): lax.psum_scatter(value.astype(jnp.bfloat16), 'fsdp', scatter_dimension=0,...]
    all_gather x4, waiting for transfers between devices: 128 us -> 166 us  [the longest x3 124 us: gather_params(): lax.all_gather(shard, 'fsdp', axis=0, tiled=True)]
    cond x128 -> x0, local copies, waits for them, and re-layouts: 29.9 us -> none
    another operation x30 -> x2, local copies, waits for them, and re-layouts: 20 us -> 2.83 us
    unnamed x36 -> x116, local copies, waits for them, and re-layouts: 1.79 us -> 18.7 us
  transfers between devices with their start and end apart: 12 -> 10, of which waited for: 10 -> 10; matrix products, arithmetic and copies ran while one was open for 4% -> 10% of each run, Pallas kernels for 0% -> 0%
where the time goes in v1:
time: 669 us; the launch traced here: 665 us
  waiting for transfers between devices  449 us (67%)
  matrix products  107 us (16%)
  local copies, waits for them, and re-layouts  58.8 us (9%)
  other arithmetic  29.7 us (4%)
  between operations  15.3 us (2%)
    reduce_scatter x4, waiting for transfers between devices, scatter_sum(): lax.psum_scatter(value.astype(jnp.bfloat16), 'fsdp', scatter_dimension=0,...  244 us
    all_gather x3, waiting for transfers between devices, gather_params(): lax.all_gather(shard, 'fsdp', axis=0, tiled=True)  124 us
    all_gather x1, waiting for transfers between devices, gather_with_vector(): lax.all_gather(jnp.concatenate([w_shard, padded], axis=0), 'fsdp', axis=0)  41.6 us
    ppermute x2, waiting for transfers between devices, shifted(): lax.ppermute(value, axis, [(source, source + steps) for source in range(f...  36.6 us
    dot_general x8, matrix products, right_dot(): lax.dot_general(left, right, (((1,), (1,)), ((), ())), preferred_element_...  32.1 us
    dot_general x4, matrix products, left_dot(): lax.dot_general(left, right, (((0,), (0,)), ((), ())), preferred_element_...  18.8 us
    unnamed x116, local copies, waits for them, and re-layouts  18.7 us
    reshape x8, local copies, waits for them, and re-layouts, rows_of(): return value.reshape(groups, value.shape[0] // groups, HEADS, HEAD)  16.3 us
  transfers between devices with their start and end apart: 10, of which 10 were waited for; matrix products, arithmetic and copies ran while one was open for 10% of the time, Pallas kernels for 0%

profile of v1, /device:TPU:0, one launch (start us, length us, event | category | flops | bytes accessed | tf_op | source)
XLA Modules:
  0.0 664.8 jit_solution(14468569929738721279)
XLA Ops:
  11.6 41.6 %all-gather.11.cloned.1.call-done = bf16[1024,768]{1,0:T(8,128)(2,1)} async-done(((bf16[64,768]{1,0:T(8,128)(2,1)}), bf16[1024,768]{1,0:T(8,128)(2,1)}) %all-gather.11.cloned.1.call-update) | async-done | bytes 1572880 | tf_op jit(solution)/shard_map/all_gather | solution.py:227
  53.3 2.4 slice.97
  56.8 44.9 %all-gather.9.cloned.1.call-done = bf16[1,768,2304]{2,1,0:T(8,128)(2,1)} async-done(((bf16[1,48,2304]{2,1,0:T(8,128)(2,1)}), bf16[1,768,2304]{2,1,0:T(8,128)(2,1)}) %all-gather.9.cloned.1.call-update) | async-done | bytes 3538960 | tf_op jit(solution)/shard_map/all_gather | solution.py:220
  101.7 4.0 fusion.28
  107.2 2.4 reshape.260
  110.8 2.2 reshape.261
  114.2 2.2 reshape.259
  123.4 32.8 %all-gather.13.cloned.1.call-done = bf16[1,768,3072]{2,1,0:T(8,128)(2,1)} async-done(((bf16[1,48,3072]{2,1,0:T(8,128)(2,1)}), bf16[1,768,3072]{2,1,0:T(8,128)(2,1)}) %all-gather.13.cloned.1.call-update) | async-done | bytes 4718608 | tf_op jit(solution)/shard_map/all_gather | solution.py:220
  156.2 7.4 %multiply_convert_fusion.4 = bf16[512,3072]{1,0:T(8,128)(2,1)} fusion(bf16[1,768,3072]{2,1,0:T(8,128)(2,1)} %all-gather.13.cloned.1.call-done, f32[3072]{0:T(1024)S(1)} %slice.101, f32[512,768]{1,0:T(8,128)S(1)} %get-tuple-element.50, f32[768]{0:T(1024)S(1)} %get-tuple-element.39, f32[768]{0:T(1024)S(1)} %get-tuple-element.40, f32[512]{0:T(512)S(1)} %add_rsqrt_fusion.3, ...), kind=kOutput, calls=%fused_computation.13 | convolution fusion | flops 2427322368 | bytes 9459712 | tf_op jit(solution)/shard_map/dot_general | solution.py:135
  163.6 46.6 %all-gather.15.cloned.1.call-done = bf16[1,3072,768]{2,1,0:T(8,128)(2,1)} async-done(((bf16[1,192,768]{2,1,0:T(8,128)(2,1)}), bf16[1,3072,768]{2,1,0:T(8,128)(2,1)}) %all-gather.15.cloned.1.call-update) | async-done | bytes 4718608 | tf_op jit(solution)/shard_map/all_gather | solution.py:220
  210.2 6.0 fusion.133
  216.9 3.4 collective-permute-start
  220.7 16.8 %collective-permute-done = bf16[512,768]{1,0:T(8,128)(2,1)S(1)} collective-permute-done((bf16[512,768]{1,0:T(8,128)(2,1)S(1)}, bf16[512,768]{1,0:T(8,128)(2,1)S(1)}, u32[]{:S(2)}, u32[]{:S(2)}) %collective-permute-start) | collective-permute-done | bytes 786464 | tf_op jit(solution)/shard_map/ppermute | solution.py:15
  237.6 4.3 fusion.26
  250.2 2.3 copy.44
  252.5 3.3 reshape.263
  255.8 2.8 bitcast_convert_fusion.2
  262.1 3.2 multiply_convert_fusion.3
  265.4 2.8 fusion.134
  271.2 4.8 multiply_convert_fusion.2
  276.0 2.9 fusion.128
  280.1 1.8 convolution_convert_fusion.9
  281.9 2.3 copy.52
  284.3 2.9 reshape.266
  287.2 2.0 fusion.55
  289.2 4.6 multiply_convert_fusion.1
  301.2 3.2 add_convert_fusion
  305.7 19.9 %collective-permute-done.1 = bf16[512,768]{1,0:T(8,128)(2,1)} collective-permute-done((bf16[512,768]{1,0:T(8,128)(2,1)}, bf16[512,768]{1,0:T(8,128)(2,1)}, u32[]{:S(2)}, u32[]{:S(2)}) %collective-permute-start.1) | collective-permute-done | bytes 786464 | tf_op jit(solution)/shard_map/ppermute | solution.py:15
  325.6 2.9 multiply_reduce_fusion
  328.5 2.0 fusion.129
  330.6 8.3 %fusion.135 = (bf16[3072]{0:T(1024)(128)(2,1)S(1)}, bf16[512,3072]{1,0:T(8,128)(2,1)S(1)}) fusion(f32[512,3072]{1,0:T(8,128)} %copy-done.39, f32[3072]{0:T(1024)S(1)} %slice.101, bf16[1,3072,768]{2,1,0:T(8,128)(2,1)} %all-gather.15.cloned.1.call-done, f32[512,768]{1,0:T(8,128)S(1)} %get-tuple-element.29), kind=kOutput, calls=%fused_computation.210 | convolution fusion | flops 2435183616 | bytes 15747072 | tf_op jit(solution)/shard_map/dot_general | solution.py:63
  339.0 3.1 multiply_reduce_fusion.1
  345.4 2.3 copy.66
  347.7 2.9 reshape.270
  350.6 3.3 bitcast_convert_fusion
  357.6 5.9 multiply_convert_fusion
  367.4 2.6 fusion.50
  370.1 2.0 copy.79
  377.2 3.8 convolution_convert_fusion.2
  382.4 6.7 %convolution_convert_fusion = bf16[3072,768]{1,0:T(8,128)(2,1)} fusion(bf16[512,3072]{1,0:T(8,128)(2,1)} %copy-done.41, f32[512,768]{1,0:T(8,128)S(1)} %copy-done.31), kind=kOutput, calls=%fused_computation.17 | convolution fusion | flops 2418671616 | bytes 9437184 | tf_op jit(solution)/shard_map/dot_general | solution.py:57
  390.6 6.5 convolution_convert_fusion.1
  398.9 6.2 add_select_fusion
  405.1 22.3 %reduce-scatter.7.cloned.1.call-done = bf16[64,768]{1,0:T(8,128)(2,1)} async-done(((bf16[1024,768]{1,0:T(8,128)(2,1)}), bf16[64,768]{1,0:T(8,128)(2,1)}) %reduce-scatter.7.cloned.1.call-update) | async-done | bytes 98320 | tf_op jit(solution)/shard_map/reduce_scatter | solution.py:233
  430.2 68.5 %reduce-scatter.5.cloned.1.call-done = bf16[48,2304]{1,0:T(8,128)(2,1)} async-done(((bf16[768,2304]{1,0:T(8,128)(2,1)}), bf16[48,2304]{1,0:T(8,128)(2,1)}) %reduce-scatter.5.cloned.1.call-update) | async-done | bytes 221200 | tf_op jit(solution)/shard_map/reduce_scatter | solution.py:233
  500.4 77.0 %reduce-scatter.11.cloned.1.call-done = bf16[192,768]{1,0:T(8,128)(2,1)} async-done(((bf16[3072,768]{1,0:T(8,128)(2,1)}), bf16[192,768]{1,0:T(8,128)(2,1)}) %reduce-scatter.11.cloned.1.call-update) | async-done | bytes 294928 | tf_op jit(solution)/shard_map/reduce_scatter | solution.py:233
  577.5 1.8 bitcast_convert_fusion.3
  579.3 76.6 %reduce-scatter.9.cloned.1.call-done = bf16[48,3072]{1,0:T(8,128)(2,1)} async-done(((bf16[768,3072]{1,0:T(8,128)(2,1)}), bf16[48,3072]{1,0:T(8,128)(2,1)}) %reduce-scatter.9.cloned.1.call-update) | async-done | bytes 294928 | tf_op jit(solution)/shard_map/reduce_scatter | solution.py:233
  655.9 1.8 bitcast_convert_fusion.4
  (216 shorter events, 67.0 us)
Async XLA Ops:
  7.2 46.1 %all-gather.11.cloned.1.call-start = ((), (), s32[]{:S(2)}) async-start(), calls=%async_computation.9 | async-start | bytes 1671168 | tf_op jit(solution)/shard_map/all_gather | solution.py:227
  8.8 92.9 %all-gather.9.cloned.1.call-start = ((), (), s32[]{:S(2)}) async-start(), calls=%async_computation.8 | async-start | bytes 3760128 | tf_op jit(solution)/shard_map/all_gather | solution.py:220
  9.5 92.1 %copy-start.4 = (bf16[1,2,1,256,768]{4,3,2,1,0:T(8,128)(2,1)S(1)}, bf16[1,2,1,256,768]{4,3,2,1,0:T(8,128)(2,1)}, u32[]{:S(2)}) copy-start(bf16[1,2,1,256,768]{4,3,2,1,0:T(8,128)(2,1)} %param.7) | copy-start | bytes 2359300
  9.6 146.7 %all-gather.13.cloned.1.call-start = ((), (), s32[]{:S(2)}) async-start(), calls=%async_computation.10 | async-start | bytes 5013504 | tf_op jit(solution)/shard_map/all_gather | solution.py:220
  10.3 199.9 %all-gather.15.cloned.1.call-start = ((), (), s32[]{:S(2)}) async-start(), calls=%async_computation.11 | async-start | bytes 5013504 | tf_op jit(solution)/shard_map/all_gather | solution.py:220
  10.9 416.5 %reduce-scatter.7.cloned.1.call-start = ((), (), s32[]{:S(2)}) async-start(), calls=%async_computation.5 | async-start | bytes 1671168 | tf_op jit(solution)/shard_map/reduce_scatter | solution.py:233
  216.9 20.6 %collective-permute-start = (bf16[512,768]{1,0:T(8,128)(2,1)S(1)}, bf16[512,768]{1,0:T(8,128)(2,1)S(1)}, u32[]{:S(2)}, u32[]{:S(2)}) collective-permute-start(bf16[512,768]{1,0:T(8,128)(2,1)S(1)} %add_convert_fusion.1), channel_id=1, source_target_pairs={{0,16},{1,17},{2,18},{3,19},{4,20},{5,21},{6,22},{7,23},{8,24},{9,... | collective-permute-start | bytes 2359304 | tf_op jit(solution)/shard_map/ppermute | solution.py:15
  237.6 4.3 copy-start.16
  244.5 1.5 copy-start.11
  246.1 2.7 copy-start
  258.6 1.5 copy-start.33
  259.5 2.6 slice-start
  259.6 1.5 copy-start.27
  260.2 1.9 slice-start.1
  261.5 3.8 slice-start.4
  262.1 16.9 %copy-start.22 = (f32[512,768]{1,0:T(8,128)}, f32[512,768]{1,0:T(8,128)S(1)}, u32[]{:S(2)}) copy-start(f32[512,768]{1,0:T(8,128)S(1)} %subtract_multiply_fusion.4) | copy-start | bytes 4718596
  262.1 3.3 slice-start.5
  265.3 2.8 copy-start.41
  265.3 5.8 copy-start.39
  268.2 2.4 copy-start.1
  268.2 1.7 copy-start.5
  287.2 2.0 copy-start.15
  287.2 2.1 copy-start.26
  289.2 4.6 copy-start.12
  298.0 2.2 copy-start.38
  298.2 2.3 copy-start.36
  299.2 2.0 copy-start.23
  304.4 21.2 %collective-permute-start.1 = (bf16[512,768]{1,0:T(8,128)(2,1)}, bf16[512,768]{1,0:T(8,128)(2,1)}, u32[]{:S(2)}, u32[]{:S(2)}) collective-permute-start(bf16[512,768]{1,0:T(8,128)(2,1)} %add_convert_fusion), channel_id=1, source_target_pairs={{16,0},{17,1},{18,2},{19,3},{20,4},{21,5},{22,6},{23,7},{24,8},{25... | collective-permute-start | bytes 2359304 | tf_op jit(solution)/shard_map/ppermute | solution.py:15
  305.7 22.8 %copy-start.2 = (f32[512,768]{1,0:T(8,128)S(1)}, f32[512,768]{1,0:T(8,128)}, u32[]{:S(2)}) copy-start(f32[512,768]{1,0:T(8,128)} %copy-done.1) | copy-start | bytes 4718596
  305.7 22.8 %copy-start.6 = (bf16[1,2,1,256,768]{4,3,2,1,0:T(8,128)(2,1)S(1)}, bf16[1,2,1,256,768]{4,3,2,1,0:T(8,128)(2,1)}, u32[]{:S(2)}) copy-start(bf16[1,2,1,256,768]{4,3,2,1,0:T(8,128)(2,1)} %param.7) | copy-start | bytes 2359300
  328.5 10.4 %slice-start.2 = ((s8[4718592]{0:T(1024)(128)(4,1)}), s8[4194304]{0:T(1024)(128)(4,1)S(1)}, s32[]{:S(2)}) async-start(s8[4718592]{0:T(1024)(128)(4,1)} %bitcast.239), calls=%async_computation.14 | async-start | bytes 8388608
  330.6 8.4 %copy-start.30 = (f32[512,768]{1,0:T(8,128)}, f32[512,768]{1,0:T(8,128)S(1)}, u32[]{:S(2)}) copy-start(f32[512,768]{1,0:T(8,128)S(1)} %get-tuple-element.29) | copy-start | bytes 4718596
  330.6 8.4 %copy-start.24 = (f32[512,768]{1,0:T(8,128)S(1)}, f32[512,768]{1,0:T(8,128)}, u32[]{:S(2)}) copy-start(f32[512,768]{1,0:T(8,128)} %copy-done.22) | copy-start | bytes 4718596
  330.6 8.4 %slice-start.3 = ((s8[4718592]{0:T(1024)(128)(4,1)}), s8[524288]{0:T(1024)(128)(4,1)S(1)}, s32[]{:S(2)}) async-start(s8[4718592]{0:T(1024)(128)(4,1)} %bitcast.239), calls=%async_computation.15 | async-start | bytes 1048576
  338.9 3.1 copy-start.40
  342.1 1.6 copy-start.34
  350.6 3.3 copy-start.7
  350.6 3.3 copy-start.14
  353.9 1.4 copy-start.20
  353.9 1.6 copy-start.28
  357.6 5.9 copy-start.13
  370.0 128.7 %reduce-scatter.5.cloned.1.call-start = ((), (), s32[]{:S(2)}) async-start(), calls=%async_computation.4 | async-start | bytes 3760128 | tf_op jit(solution)/shard_map/reduce_scatter | solution.py:233
  370.1 2.2 copy-start.10
  375.6 1.5 copy-start.18
  381.0 1.4 copy-start.31
  381.0 196.5 %reduce-scatter.11.cloned.1.call-start = ((), (), s32[]{:S(2)}) async-start(), calls=%async_computation.7 | async-start | bytes 5013504 | tf_op jit(solution)/shard_map/reduce_scatter | solution.py:233
  389.2 266.7 %reduce-scatter.9.cloned.1.call-start = ((), (), s32[]{:S(2)}) async-start(), calls=%async_computation.6 | async-start | bytes 5013504 | tf_op jit(solution)/shard_map/reduce_scatter | solution.py:233
  397.0 1.9 copy-start.21
  (10 other events, 12.1 us)
Sparse Core Ops, SparseCore 0:
  10.9 42.3 all-gather.10
  55.5 46.0 all-gather.8
  103.9 52.2 all-gather.12
  158.3 51.8 all-gather.14
  370.2 57.1 reduce-scatter.6
  431.6 67.0 reduce-scatter.4
  503.1 74.3 reduce-scatter.10
  581.3 74.5 reduce-scatter.8

commit v2 on v1

--- a/solution.py
+++ b/solution.py
@@ -216,35 +216,55 @@
     return (grad_x, grad_vec, operands)
 
 
+def column_blocks(matrix):
+    return [matrix[:, start : start + D] for start in range(0, matrix.shape[1], D)]
+
+
+def pack_shards(w_qkv, w_out, w_up, w_down, vec):
+    padded = jnp.pad(vec[None, :], ((0, 15), (0, D - vec.shape[0])))
+    blocks = [*column_blocks(w_qkv), *column_blocks(w_up), w_out, w_down, padded]
+    return jnp.concatenate(blocks, axis=0)
+
+
+def unpack_params(packed, rows, down_rows, share):
+    count = packed.shape[0]
+
+    def block(index, height=rows):
+        return packed[:, index * rows : index * rows + height].reshape(count * height, D)
+
+    full_qkv = jnp.concatenate([block(index) for index in range(3)], axis=1)
+    full_up = jnp.concatenate([block(index) for index in range(3, 7)], axis=1)
+    vec = packed[:, 8 * rows + down_rows, :share].reshape(-1)
+    return full_qkv, block(7), full_up, block(8, down_rows), vec
+
+
 def gather_params(shards):
-    return tuple(lax.all_gather(shard, "fsdp", axis=0, tiled=True) for shard in shards)
-
-
-def gather_with_vector(w_shard, vec_shard):
+    packed = lax.all_gather(pack_shards(*shards), "fsdp", axis=0)
+    return unpack_params(packed, shards[1].shape[0], shards[3].shape[0], shards[4].shape[0])
+
+
+def scatter_grads(operands, vec_grad):
     count = lax.axis_size("fsdp")
-    rows, width = w_shard.shape
-    padded = jnp.pad(vec_shard[None, :], ((0, 15), (0, width - vec_shard.shape[0])))
-    joined = lax.all_gather(jnp.concatenate([w_shard, padded], axis=0), "fsdp", axis=0)
-    weight = joined[:, :rows].reshape(count * rows, width)
-    return weight, joined[:, rows, : vec_shard.shape[0]].reshape(-1)
-
-
-def scatter_sum(value):
-    total = lax.psum_scatter(
-        value.astype(jnp.bfloat16), "fsdp", scatter_dimension=0, tiled=True
-    )
-    return total.astype(jnp.float32)
-
-
-def scatter_with_vector(w_grad, vec_grad):
-    count = lax.axis_size("fsdp")
-    width = w_grad.shape[1]
-    rows = w_grad.shape[0] // count
+    qkv_pair, out_pair, up_pair, down_pair = operands
     share = vec_grad.shape[0] // count
-    padded = jnp.pad(vec_grad.reshape(count, 1, share), ((0, 0), (0, 15), (0, width - share)))
-    joined = jnp.concatenate([w_grad.reshape(count, rows, width), padded], axis=1)
-    total = scatter_sum(joined.reshape(-1, width))
-    return total[:rows], total[rows, :share]
+    rows = D // count
+    blocks = [left_dot(qkv_pair[0], block) for block in column_blocks(qkv_pair[1])]
+    blocks += [left_dot(up_pair[0], block) for block in column_blocks(up_pair[1])]
+    blocks += [left_dot(*out_pair), left_dot(*down_pair)]
+    blocks = [block.astype(jnp.bfloat16).reshape(count, -1, D) for block in blocks]
+    vec_block = vec_grad.astype(jnp.bfloat16).reshape(count, 1, share)
+    blocks.append(jnp.pad(vec_block, ((0, 0), (0, 15), (0, D - share))))
+    packed = jnp.concatenate(blocks, axis=1)
+    total = lax.psum_scatter(packed, "fsdp", scatter_dimension=0).astype(jnp.float32)
+    pieces = [total[index * rows : (index + 1) * rows] for index in range(8)]
+    last = total.shape[0] - 16
+    return (
+        jnp.concatenate(pieces[:3], axis=1),
+        pieces[7],
+        jnp.concatenate(pieces[3:7], axis=1),
+        total[8 * rows : last],
+        total[last, :share],
+    )
 
 
 def body(ends, lengths, w_qkv, w_out, w_up, w_down, vectors):
@@ -253,9 +273,7 @@
     local_rows = ends[0, :, 0].reshape(micro * row_count, D)
     positions = jnp.arange(row_count, dtype=jnp.int32)
     visible = positions[None, :] < lengths[:, 0][:, None]
-    full_out, full_vec = gather_with_vector(w_out[0], vectors[0])
-    full_qkv, full_up, full_down = gather_params((w_qkv[0], w_up[0], w_down[0]))
-    params = (full_qkv, full_out, full_up, full_down, full_vec)
+    params = gather_params((w_qkv[0], w_out[0], w_up[0], w_down[0], vectors[0]))
     early, _ = layer_forward(local_rows, visible, params)
     received = shifted(early.astype(jnp.bfloat16), "section", 1)
     x_in = jnp.where(is_first, local_rows, received)
@@ -266,10 +284,7 @@
     back_received = shifted(early_grad.astype(jnp.bfloat16), "section", -1)
     d_out = jnp.where(is_first, back_received.astype(jnp.float32), cotangent)
     grad_x, grad_vec, operands = layer_backward(d_out, kept_state, visible, params)
-    grad_down = scatter_sum(left_dot(*operands[3]))
-    grad_up = scatter_sum(left_dot(*operands[2]))
-    grad_qkv = scatter_sum(left_dot(*operands[0]))
-    grad_out, grad_vectors = scatter_with_vector(left_dot(*operands[1]), grad_vec)
+    grad_qkv, grad_out, grad_up, grad_down, grad_vectors = scatter_grads(operands, grad_vec)
     ends_out = jnp.where(is_first, grad_x, result).reshape(1, micro, 1, row_count, D)
     return (
         ends_out,

time: 669 us -> 552 us (0.83)
  waiting for transfers between devices: 449 us -> 288 us
  local copies, waits for them, and re-layouts: 58.8 us -> 94.6 us
  matrix products: 107 us -> 115 us
    reduce_scatter x4 -> x1, waiting for transfers between devices: 244 us -> 138 us  [scatter_grads(): lax.psum_scatter(packed, 'fsdp', scatter_dimension=0).astype(jnp.float32)]
    all_gather x4 -> x1, waiting for transfers between devices: 166 us -> 115 us  [gather_params(): packed = lax.all_gather(pack_shards(*shards), 'fsdp', axis=0)]
    unnamed x116 -> x220, local copies, waits for them, and re-layouts: 18.7 us -> 53.1 us
    slice x2 -> x7, local copies, waits for them, and re-layouts: 3.66 us -> 14.8 us  [the longest x2 11.3 us: block(): packed[:, index * rows:index * rows + height].reshape(count * height, D)]
    dot_general x8 -> x7, matrix products: 32.1 us -> 42.3 us  [right_dot(): lax.dot_general(left, right, (((1,), (1,)), ((), ())), preferred_element_...]
    dot_general x4 -> x9, matrix products: 18.8 us -> 18.3 us  [left_dot(): lax.dot_general(left, right, (((0,), (0,)), ((), ())), preferred_element_...]
  transfers between devices with their start and end apart: 10 -> 4, of which waited for: 10 -> 4; matrix products, arithmetic and copies ran while one was open for 10% -> 2% of each run, Pallas kernels for 0% -> 0%
where the time goes in v2:
time: 552 us; the launch traced here: 546 us
  waiting for transfers between devices  288 us (52%)
  matrix products  115 us (21%)
  local copies, waits for them, and re-layouts  94.6 us (17%)
  other arithmetic  28 us (5%)
  between operations  15.9 us (3%)
    reduce_scatter x1, waiting for transfers between devices, scatter_grads(): lax.psum_scatter(packed, 'fsdp', scatter_dimension=0).astype(jnp.float32)  138 us
    all_gather x1, waiting for transfers between devices, gather_params(): packed = lax.all_gather(pack_shards(*shards), 'fsdp', axis=0)  115 us
    unnamed x220, local copies, waits for them, and re-layouts  53.1 us
    dot_general x7, matrix products, right_dot(): lax.dot_general(left, right, (((1,), (1,)), ((), ())), preferred_element_...  42.3 us
    ppermute x2, waiting for transfers between devices, shifted(): lax.ppermute(value, axis, [(source, source + steps) for source in range(f...  34.1 us
    dot_general x9, matrix products, left_dot(): lax.dot_general(left, right, (((0,), (0,)), ((), ())), preferred_element_...  18.3 us
    dot_general x2, matrix products, layer_forward(): jnp.dot(act_b, w_down, preferred_element_type=jnp.float32)  13 us
    reshape x8, local copies, waits for them, and re-layouts, rows_of(): return value.reshape(groups, value.shape[0] // groups, HEADS, HEAD)  12.1 us
  transfers between devices with their start and end apart: 4, of which 4 were waited for; matrix products, arithmetic and copies ran while one was open for 2% of the time, Pallas kernels for 0%

profile of v2, /device:TPU:0, one launch (start us, length us, event | category | flops | bytes accessed | tf_op | source)
XLA Modules:
  0.0 546.2 jit_solution(14067832635609288866)
XLA Ops:
  17.0 115.2 %all-gather.3.cloned.1.call-done = bf16[9472,768]{1,0:T(8,128)(2,1)} async-done(((bf16[592,768]{1,0:T(8,128)(2,1)}), bf16[9472,768]{1,0:T(8,128)(2,1)}) %all-gather.3.cloned.1.call-update) | async-done | bytes 14549008 | tf_op jit(solution)/shard_map/all_gather | solution.py:242
  133.2 4.9 slice.257
  139.4 6.4 %fusion.122 = (bf16[16,48,768]{2,1,0:T(8,128)(2,1)}, bf16[16,48,768]{2,1,0:T(8,128)(2,1)}, bf16[16,48,768]{2,1,0:T(8,128)(2,1)}, bf16[16,48,768]{2,1,0:T(8,128)(...) fusion(bf16[16,592,768]{2,1,0:T(8,128)(2,1)} %bitcast.189), kind=kLoop, calls=%fused_computation.229 | loop fusion | bytes 18874368 | tf_op jit(solution)/shard_map/slice | solution.py:233
  145.9 2.0 convolution_bitcast_fusion
  147.9 2.1 copy-done.28
  150.4 3.0 fusion.33
  153.4 2.2 reshape.330
  155.6 1.7 fusion.4
  160.2 4.2 fusion.42
  168.5 10.3 %fusion.127 = (f32[512]{0:T(512)}, f32[512,768]{1,0:T(8,128)S(1)}) fusion(f32[768]{0:T(1024)} %get-tuple-element.59, bf16[3072,768]{1,0:T(8,128)(2,1)} %bitcast.191, f32[3072]{0:T(1024)} %slice.256, f32[512,768]{1,0:T(8,128)} %copy-done.36, f32[768]{0:T(1024)} %get-tuple-element.60, f32[768]{0:T(1024)} %get-tuple-element.61, f32[512]{0:T(512)} %add_rsqrt_fusion.3, ...), kind=kOutput, calls=%fused_computation.234 | convolution fusion | flops 4864867840 | bytes 12610560 | tf_op jit(solution)/shard_map/dot_general | solution.py:137
  181.0 3.6 collective-permute-start
  187.6 14.3 %collective-permute-done = bf16[512,768]{1,0:T(8,128)(2,1)S(1)} collective-permute-done((bf16[512,768]{1,0:T(8,128)(2,1)}, bf16[512,768]{1,0:T(8,128)(2,1)S(1)}, u32[]{:S(2)}, u32[]{:S(2)}) %collective-permute-start) | collective-permute-done | bytes 786464 | tf_op jit(solution)/shard_map/ppermute | solution.py:15
  202.1 2.0 fusion.117
  206.0 3.3 copy.92
  210.9 3.0 add_convert_fusion.1
  219.9 3.3 reshape.338
  223.2 2.8 bitcast_convert_fusion.2
  231.6 7.5 %multiply_convert_fusion.3 = (bf16[512,3072]{1,0:T(8,128)(2,1)S(1)}, f32[512,3072]{1,0:T(8,128)}) fusion(f32[3072]{0:T(1024)S(1)} %copy-done.76, bf16[512,768]{1,0:T(8,128)(2,1)S(1)} %get-tuple-element.32, bf16[768,768]{1,0:T(8,128)(2,1)S(1)} %bitcast.230, bf16[768,768]{1,0:T(8,128)(2,1)S(1)} %bitcast.234, bf16[768,768]{1,0:T(8,128)(2,1)S(1)} %bitcast.238, ...), kind=kOutput, calls=%fused_computation.8 | convolution fusion | flops 2444230656 | bytes 14954496 | tf_op jit(solution)/shard_map/dot_general | solution.py:135
  239.2 2.7 fusion.130
  244.4 14.2 %fusion.119 = (f32[512]{0:T(512)S(1)}, f32[512]{0:T(512)S(1)}, f32[512,768]{1,0:T(8,128)}) fusion(f32[512,768]{1,0:T(8,128)} %copy-done.24, f32[768]{0:T(1024)S(1)} %copy-done.71, bf16[768,768]{1,0:T(8,128)(2,1)} %bitcast.229, bf16[768,768]{1,0:T(8,128)(2,1)} %bitcast.233, bf16[768,768]{1,0:T(8,128)(2,1)} %bitcast.237, bf16[768,768]{1,0:T(8,128)(2,1)} %bitcast.224, ...), kind=kOutput, calls=%fused_computation.226 | convolution fusion | flops 4877450240 | bytes 21266432 | tf_op jit(solution)/shard_map/dot_general | solution.py:63
  258.7 4.0 convolution_convert_fusion.14
  262.7 2.3 copy.51
  265.0 2.9 reshape.341
  267.9 2.3 fusion.45
  271.4 4.7 multiply_convert_fusion.1
  281.9 3.2 add_convert_fusion
  286.4 19.8 %collective-permute-done.1 = bf16[512,768]{1,0:T(8,128)(2,1)} collective-permute-done((bf16[512,768]{1,0:T(8,128)(2,1)}, bf16[512,768]{1,0:T(8,128)(2,1)}, u32[]{:S(2)}, u32[]{:S(2)}) %collective-permute-start.1) | collective-permute-done | bytes 786464 | tf_op jit(solution)/shard_map/ppermute | solution.py:15
  306.2 2.1 multiply_reduce_fusion
  308.3 1.9 fusion.120
  310.3 8.1 %fusion.123 = (bf16[3072]{0:T(1024)(128)(2,1)S(1)}, bf16[512,3072]{1,0:T(8,128)(2,1)S(1)}) fusion(f32[512,3072]{1,0:T(8,128)} %get-tuple-element.81, f32[3072]{0:T(1024)S(1)} %copy-done.76, bf16[3072,768]{1,0:T(8,128)(2,1)} %bitcast.193, f32[512,768]{1,0:T(8,128)S(1)} %get-tuple-element.29), kind=kOutput, calls=%fused_computation.230 | convolution fusion | flops 2435183616 | bytes 15747072 | tf_op jit(solution)/shard_map/dot_general | solution.py:63
  318.4 4.4 multiply_reduce_fusion.1
  324.4 1.7 convolution_convert_fusion.10
  326.1 2.4 copy.65
  328.5 2.9 reshape.345
  331.5 4.5 bitcast_convert_fusion
  337.6 2.8 multiply_convert_fusion
  343.6 1.8 convolution_convert_fusion.5
  345.5 1.8 convolution_convert_fusion.4
  347.3 1.8 convolution_convert_fusion.3
  349.1 1.8 convolution_convert_fusion.2
  350.9 1.9 convolution_convert_fusion.1
  352.8 4.7 convolution_convert_fusion
  362.9 1.8 convolution_convert_fusion.7
  364.7 1.9 convolution_convert_fusion.6
  370.6 2.4 constant_dynamic-update-slice_fusion.8
  381.4 5.0 constant_dynamic-update-slice_fusion.1
  388.5 6.7 %add_select_fusion = f32[512,768]{1,0:T(8,128)} fusion(f32[512,768]{1,0:T(8,128)S(1)} %copy-done.22, bf16[512,768]{0,1:T(8,128)(2,1)} %bitcast.248, bf16[512,768]{0,1:T(8,128)(2,1)} %bitcast.250, bf16[512,768]{0,1:T(8,128)(2,1)} %bitcast.252, f32[768]{0:T(1024)S(1)} %copy-done.74, f32[768]{0:T(1024)S(1)} %get-tuple-element.57, pred[]{:T(512)S(6)} %eq.3, ...), kind=kOutput, calls=%fused_computation.69 | convolution fusion | flops 1831993344 | bytes 10627073 | tf_op jit(solution)/shard_map/dot_general | solution.py:63
  395.3 138.3 %reduce-scatter.2.cloned.1.call-done = bf16[1,592,768]{2,1,0:T(8,128)(2,1)} async-done(((bf16[16,592,768]{2,1,0:T(8,128)(2,1)}), bf16[1,592,768]{2,1,0:T(8,128)(2,1)}) %reduce-scatter.2.cloned.1.call-update) | async-done | bytes 909328 | tf_op jit(solution)/shard_map/reduce_scatter | solution.py:258
  (301 shorter events, 81.4 us)
Async XLA Ops:
  7.2 8.2 %copy-start.79 = (bf16[1,576]{1,0:T(2,128)(2,1)S(1)}, bf16[1,576]{1,0:T(2,128)(2,1)}, u32[]{:S(2)}) copy-start(bf16[1,576]{1,0:T(2,128)(2,1)} %param.13) | copy-start | bytes 3460
  7.2 9.2 %copy-start.81 = (s32[2,1]{0,1:T(1,128)S(1)}, s32[2,1]{0,1:T(1,128)}, u32[]{:S(2)}) copy-start(s32[2,1]{0,1:T(1,128)} %param.8) | copy-start | bytes 28
  7.2 125.0 %all-gather.3.cloned.1.call-start = ((), (), s32[]{:S(2)}) async-start(), calls=%async_computation.2 | async-start | bytes 15458304 | tf_op jit(solution)/shard_map/all_gather | solution.py:242
  16.3 517.2 %reduce-scatter.2.cloned.1.call-start = ((), (), s32[]{:S(2)}) async-start(), calls=%async_computation.1 | async-start | bytes 15458304 | tf_op jit(solution)/shard_map/reduce_scatter | solution.py:258
  138.8 11.6 %copy-start.69 = (f32[768]{0:T(1024)}, f32[768]{0:T(1024)S(1)}, u32[]{:S(2)}) copy-start(f32[768]{0:T(1024)S(1)} %get-tuple-element.64) | copy-start | bytes 9220
  139.4 6.5 %copy-start.6 = (bf16[1,2,1,256,768]{4,3,2,1,0:T(8,128)(2,1)S(1)}, bf16[1,2,1,256,768]{4,3,2,1,0:T(8,128)(2,1)}, u32[]{:S(2)}) copy-start(bf16[1,2,1,256,768]{4,3,2,1,0:T(8,128)(2,1)} %param.7) | copy-start | bytes 2359300
  147.9 2.1 copy-start.28
  157.3 2.6 copy-start.5
  179.8 22.2 %copy-start.44 = (bf16[16,48,768]{2,1,0:T(8,128)(2,1)S(1)}, bf16[16,48,768]{2,1,0:T(8,128)(2,1)}, u32[]{:S(2)}) copy-start(bf16[16,48,768]{2,1,0:T(8,128)(2,1)} %copy-done.43) | copy-start | bytes 3538948
  181.0 20.9 %collective-permute-start = (bf16[512,768]{1,0:T(8,128)(2,1)}, bf16[512,768]{1,0:T(8,128)(2,1)S(1)}, u32[]{:S(2)}, u32[]{:S(2)}) collective-permute-start(bf16[512,768]{1,0:T(8,128)(2,1)} %add_convert_fusion.3), channel_id=1, source_target_pairs={{0,16},{1,17},{2,18},{3,19},{4,20},{5,21},{6,22},{7,23},{8,24},{9,... | collective-permute-start | bytes 2359304 | tf_op jit(solution)/shard_map/ppermute | solution.py:15
  185.8 16.2 %copy-start.38 = (bf16[16,48,768]{2,1,0:T(8,128)(2,1)S(1)}, bf16[16,48,768]{2,1,0:T(8,128)(2,1)}, u32[]{:S(2)}) copy-start(bf16[16,48,768]{2,1,0:T(8,128)(2,1)} %copy-done.37) | copy-start | bytes 3538948
  185.8 16.2 %copy-start.41 = (bf16[16,48,768]{2,1,0:T(8,128)(2,1)S(1)}, bf16[16,48,768]{2,1,0:T(8,128)(2,1)}, u32[]{:S(2)}) copy-start(bf16[16,48,768]{2,1,0:T(8,128)(2,1)} %copy-done.40) | copy-start | bytes 3538948
  206.0 8.2 %copy-start.11 = (bf16[2,256,12,64]{1,0,3,2:T(2,128)(2,1)}, bf16[2,256,12,64]{1,0,3,2:T(2,128)(2,1)S(1)}, u32[]{:S(2)}) copy-start(bf16[2,256,12,64]{1,0,3,2:T(2,128)(2,1)S(1)} %reshape.340) | copy-start | bytes 2359300
  215.8 2.7 copy-start
  219.9 48.0 %copy-start.1 = (bf16[2,12,256,256]{2,3,1,0:T(8,128)(2,1)}, bf16[2,12,256,256]{2,3,1,0:T(8,128)(2,1)S(1)}, u32[]{:S(2)}) copy-start(bf16[2,12,256,256]{2,3,1,0:T(8,128)(2,1)S(1)} %fusion.6) | copy-start | bytes 9437188
  228.6 3.0 copy-start.56
  228.6 3.0 copy-start.76
  229.2 10.0 %slice-start.2 = ((s8[4718592]{0:T(1024)(128)(4,1)}), s8[4194304]{0:T(1024)(128)(4,1)S(1)}, s32[]{:S(2)}) async-start(s8[4718592]{0:T(1024)(128)(4,1)} %bitcast.194), calls=%async_computation.5 | async-start | bytes 8388608
  229.6 9.5 %copy-start.64 = (bf16[512,768]{1,0:T(8,128)(2,1)}, bf16[512,768]{1,0:T(8,128)(2,1)S(1)}, u32[]{:S(2)}) copy-start(bf16[512,768]{1,0:T(8,128)(2,1)S(1)} %get-tuple-element.32) | copy-start | bytes 2359300
  229.6 9.5 %copy-start.24 = (f32[512,768]{1,0:T(8,128)}, f32[512,768]{1,0:T(8,128)S(1)}, u32[]{:S(2)}) copy-start(f32[512,768]{1,0:T(8,128)S(1)} %get-tuple-element.33) | copy-start | bytes 4718596
  231.6 7.6 %slice-start.3 = ((s8[4718592]{0:T(1024)(128)(4,1)}), s8[524288]{0:T(1024)(128)(4,1)S(1)}, s32[]{:S(2)}) async-start(s8[4718592]{0:T(1024)(128)(4,1)} %bitcast.194), calls=%async_computation.6 | async-start | bytes 1048576
  231.6 7.6 %copy-start.78 = (f32[768]{0:T(1024)S(1)}, f32[768]{0:T(1024)}, u32[]{:S(2)}) copy-start(f32[768]{0:T(1024)} %get-tuple-element.59) | copy-start | bytes 9220
  239.2 2.8 copy-start.85
  242.0 2.4 copy-start.2
  267.9 2.4 copy-start.9
  267.9 2.4 copy-start.20
  271.4 4.7 copy-start.14
  278.7 2.2 copy-start.82
  281.9 24.3 %copy-start.3 = (f32[512,768]{1,0:T(8,128)S(1)}, f32[512,768]{1,0:T(8,128)}, u32[]{:S(2)}) copy-start(f32[512,768]{1,0:T(8,128)} %copy-done.2) | copy-start | bytes 4718596
  281.9 24.3 %copy-start.8 = (bf16[1,2,1,256,768]{4,3,2,1,0:T(8,128)(2,1)S(1)}, bf16[1,2,1,256,768]{4,3,2,1,0:T(8,128)(2,1)}, u32[]{:S(2)}) copy-start(bf16[1,2,1,256,768]{4,3,2,1,0:T(8,128)(2,1)} %param.7) | copy-start | bytes 2359300
  285.1 21.1 %collective-permute-start.1 = (bf16[512,768]{1,0:T(8,128)(2,1)}, bf16[512,768]{1,0:T(8,128)(2,1)}, u32[]{:S(2)}, u32[]{:S(2)}) collective-permute-start(bf16[512,768]{1,0:T(8,128)(2,1)} %add_convert_fusion), channel_id=1, source_target_pairs={{16,0},{17,1},{18,2},{19,3},{20,4},{21,5},{22,6},{23,7},{24,8},{25... | collective-permute-start | bytes 2359304 | tf_op jit(solution)/shard_map/ppermute | solution.py:15
  310.2 8.2 %copy-start.34 = (f32[512,768]{1,0:T(8,128)}, f32[512,768]{1,0:T(8,128)S(1)}, u32[]{:S(2)}) copy-start(f32[512,768]{1,0:T(8,128)S(1)} %get-tuple-element.29) | copy-start | bytes 4718596
  310.2 8.2 %copy-start.26 = (f32[512,768]{1,0:T(8,128)S(1)}, f32[512,768]{1,0:T(8,128)}, u32[]{:S(2)}) copy-start(f32[512,768]{1,0:T(8,128)} %copy-done.24) | copy-start | bytes 4718596
  310.3 8.2 %copy-start.51 = (bf16[16,48,768]{2,1,0:T(8,128)(2,1)S(1)}, bf16[16,48,768]{2,1,0:T(8,128)(2,1)}, u32[]{:S(2)}) copy-start(bf16[16,48,768]{2,1,0:T(8,128)(2,1)} %get-tuple-element.34) | copy-start | bytes 3538948
  310.3 8.2 %copy-start.53 = (bf16[16,48,768]{2,1,0:T(8,128)(2,1)S(1)}, bf16[16,48,768]{2,1,0:T(8,128)(2,1)}, u32[]{:S(2)}) copy-start(bf16[16,48,768]{2,1,0:T(8,128)(2,1)} %get-tuple-element.35) | copy-start | bytes 3538948
  310.3 8.2 %copy-start.55 = (bf16[16,48,768]{2,1,0:T(8,128)(2,1)S(1)}, bf16[16,48,768]{2,1,0:T(8,128)(2,1)}, u32[]{:S(2)}) copy-start(bf16[16,48,768]{2,1,0:T(8,128)(2,1)} %get-tuple-element.36) | copy-start | bytes 3538948
  310.3 8.2 %copy-start.57 = (bf16[16,48,768]{2,1,0:T(8,128)(2,1)S(1)}, bf16[16,48,768]{2,1,0:T(8,128)(2,1)}, u32[]{:S(2)}) copy-start(bf16[16,48,768]{2,1,0:T(8,128)(2,1)} %get-tuple-element.37) | copy-start | bytes 3538948
  318.4 4.4 copy-start.83
  326.1 11.4 %slice-start = ((s8[6291456]{0:T(1024)(128)(4,1)}), s8[2097152]{0:T(1024)(128)(4,1)S(1)}, s32[]{:S(2)}) async-start(s8[6291456]{0:T(1024)(128)(4,1)} %bitcast.182), calls=%async_computation.3 | async-start | bytes 4194304
  331.5 4.5 copy-start.10
  331.5 6.1 %slice-start.1 = ((s8[6291456]{0:T(1024)(128)(4,1)}), s8[4194304]{0:T(1024)(128)(4,1)S(1)}, s32[]{:S(2)}) async-start(s8[6291456]{0:T(1024)(128)(4,1)} %bitcast.182), calls=%async_computation.4 | async-start | bytes 8388608
  337.6 2.8 copy-start.15
  341.5 2.1 copy-start.84
  349.1 3.7 copy-start.86
  358.5 6.3 %copy-start.66 = (bf16[96,8,2,256]{3,1,2,0:T(8,128)(2,1)}, bf16[96,8,2,256]{3,1,2,0:T(8,128)(2,1)S(1)}, u32[]{:S(2)}) copy-start(bf16[96,8,2,256]{3,1,2,0:T(8,128)(2,1)S(1)} %copy.103) | copy-start | bytes 2359300
  359.5 3.4 copy-start.67
  368.2 4.8 copy-start.62
  535.0 2.3 copy-start.33
  (47 other events, 72.0 us)
Sparse Core Ops, SparseCore 0:
  16.4 115.7 all-gather.2
  387.3 146.2 reduce-scatter.1

commit v3 on v2

--- a/solution.py
+++ b/solution.py
@@ -243,27 +243,34 @@
     return unpack_params(packed, shards[1].shape[0], shards[3].shape[0], shards[4].shape[0])
 
 
+def scatter_blocks(blocks):
+    count = lax.axis_size("fsdp")
+    blocks = [block.astype(jnp.bfloat16).reshape(count, -1, block.shape[-1]) for block in blocks]
+    packed = jnp.concatenate(blocks, axis=1)
+    return lax.psum_scatter(packed, "fsdp", scatter_dimension=0).astype(jnp.float32)
+
+
+def joined_columns(total, rows, blocks):
+    pieces = [total[index * rows : (index + 1) * rows] for index in range(blocks)]
+    return jnp.concatenate(pieces, axis=1)
+
+
 def scatter_grads(operands, vec_grad):
     count = lax.axis_size("fsdp")
     qkv_pair, out_pair, up_pair, down_pair = operands
     share = vec_grad.shape[0] // count
     rows = D // count
+    up_blocks = [left_dot(up_pair[0], block) for block in column_blocks(up_pair[1])]
+    mlp_total = scatter_blocks([*up_blocks, left_dot(*down_pair)])
     blocks = [left_dot(qkv_pair[0], block) for block in column_blocks(qkv_pair[1])]
-    blocks += [left_dot(up_pair[0], block) for block in column_blocks(up_pair[1])]
-    blocks += [left_dot(*out_pair), left_dot(*down_pair)]
-    blocks = [block.astype(jnp.bfloat16).reshape(count, -1, D) for block in blocks]
-    vec_block = vec_grad.astype(jnp.bfloat16).reshape(count, 1, share)
-    blocks.append(jnp.pad(vec_block, ((0, 0), (0, 15), (0, D - share))))
-    packed = jnp.concatenate(blocks, axis=1)
-    total = lax.psum_scatter(packed, "fsdp", scatter_dimension=0).astype(jnp.float32)
-    pieces = [total[index * rows : (index + 1) * rows] for index in range(8)]
-    last = total.shape[0] - 16
+    vec_block = jnp.pad(vec_grad.reshape(count, 1, share), ((0, 0), (0, 15), (0, D - share)))
+    rest = scatter_blocks([*blocks, left_dot(*out_pair), vec_block])
     return (
-        jnp.concatenate(pieces[:3], axis=1),
-        pieces[7],
-        jnp.concatenate(pieces[3:7], axis=1),
-        total[8 * rows : last],
-        total[last, :share],
+        joined_columns(rest, rows, 3),
+        rest[3 * rows : 4 * rows],
+        joined_columns(mlp_total, rows, 4),
+        mlp_total[4 * rows :],
+        rest[4 * rows, :share],
     )
 
 

time: 552 us -> 569 us (1.031)
  waiting for transfers between devices: 288 us -> 310 us
  matrix products: 115 us -> 109 us
    reduce_scatter x1 -> x2, waiting for transfers between devices: 138 us -> 161 us  [scatter_blocks(): lax.psum_scatter(packed, 'fsdp', scatter_dimension=0).astype(jnp.float32)]
    unnamed x220 -> x211, local copies, waits for them, and re-layouts: 53.1 us -> 49 us
  transfers between devices with their start and end apart: 4 -> 5, of which waited for: 4 -> 5; matrix products, arithmetic and copies ran while one was open for 2% -> 5% of each run, Pallas kernels for 0% -> 0%
where the time goes in v3:
time: 569 us; the launch traced here: 562 us
  waiting for transfers between devices  310 us (54%)
  matrix products  109 us (19%)
  local copies, waits for them, and re-layouts  93.8 us (16%)
  other arithmetic  28.8 us (5%)
  between operations  15.6 us (3%)
    reduce_scatter x2, waiting for transfers between devices, scatter_blocks(): lax.psum_scatter(packed, 'fsdp', scatter_dimension=0).astype(jnp.float32)  161 us
    all_gather x1, waiting for transfers between devices, gather_params(): packed = lax.all_gather(pack_shards(*shards), 'fsdp', axis=0)  115 us
    unnamed x211, local copies, waits for them, and re-layouts  49 us
    dot_general x7, matrix products, right_dot(): lax.dot_general(left, right, (((1,), (1,)), ((), ())), preferred_element_...  41.7 us
    ppermute x2, waiting for transfers between devices, shifted(): lax.ppermute(value, axis, [(source, source + steps) for source in range(f...  34 us
    dot_general x2, matrix products, layer_forward(): jnp.dot(act_b, w_down, preferred_element_type=jnp.float32)  12.9 us
    dot_general x9, matrix products, left_dot(): lax.dot_general(left, right, (((0,), (0,)), ((), ())), preferred_element_...  12.7 us
    reshape x8, local copies, waits for them, and re-layouts, rows_of(): return value.reshape(groups, value.shape[0] // groups, HEADS, HEAD)  12.1 us
  transfers between devices with their start and end apart: 5, of which 5 were waited for; matrix products, arithmetic and copies ran while one was open for 5% of the time, Pallas kernels for 0%

profile of v3, /device:TPU:0, one launch (start us, length us, event | category | flops | bytes accessed | tf_op | source)
XLA Modules:
  0.0 562.5 jit_solution(993619912837391832)
XLA Ops:
  17.0 115.2 %all-gather.3.cloned.1.call-done = bf16[9472,768]{1,0:T(8,128)(2,1)} async-done(((bf16[592,768]{1,0:T(8,128)(2,1)}), bf16[9472,768]{1,0:T(8,128)(2,1)}) %all-gather.3.cloned.1.call-update) | async-done | bytes 14549008 | tf_op jit(solution)/shard_map/all_gather | solution.py:242
  133.2 4.9 slice.257
  139.4 6.5 %fusion.122 = (bf16[16,48,768]{2,1,0:T(8,128)(2,1)}, bf16[16,48,768]{2,1,0:T(8,128)(2,1)}, bf16[16,48,768]{2,1,0:T(8,128)(2,1)}, bf16[16,48,768]{2,1,0:T(8,128)(...) fusion(bf16[16,592,768]{2,1,0:T(8,128)(2,1)} %bitcast.189), kind=kLoop, calls=%fused_computation.229 | loop fusion | bytes 18874368 | tf_op jit(solution)/shard_map/slice | solution.py:233
  145.9 2.1 convolution_bitcast_fusion
  148.0 2.1 copy-done.28
  150.4 3.0 fusion.33
  153.5 2.2 reshape.323
  155.7 1.7 fusion.4
  160.3 4.2 fusion.42
  168.6 10.2 %fusion.127 = (f32[512]{0:T(512)}, f32[512,768]{1,0:T(8,128)S(1)}) fusion(f32[768]{0:T(1024)} %get-tuple-element.59, bf16[3072,768]{1,0:T(8,128)(2,1)} %bitcast.191, f32[3072]{0:T(1024)} %slice.256, f32[512,768]{1,0:T(8,128)} %copy-done.36, f32[768]{0:T(1024)} %get-tuple-element.60, f32[768]{0:T(1024)} %get-tuple-element.61, f32[512]{0:T(512)} %add_rsqrt_fusion.3, ...), kind=kOutput, calls=%fused_computation.234 | convolution fusion | flops 4864867840 | bytes 12610560 | tf_op jit(solution)/shard_map/dot_general | solution.py:137
  180.9 3.6 collective-permute-start
  187.6 14.2 %collective-permute-done = bf16[512,768]{1,0:T(8,128)(2,1)S(1)} collective-permute-done((bf16[512,768]{1,0:T(8,128)(2,1)}, bf16[512,768]{1,0:T(8,128)(2,1)S(1)}, u32[]{:S(2)}, u32[]{:S(2)}) %collective-permute-start) | collective-permute-done | bytes 786464 | tf_op jit(solution)/shard_map/ppermute | solution.py:15
  202.0 2.0 fusion.117
  205.9 3.3 copy.92
  209.2 1.6 copy.91
  210.9 3.0 add_convert_fusion.1
  214.1 1.6 fusion.5
  219.8 3.3 reshape.331
  223.1 2.8 bitcast_convert_fusion.2
  231.5 7.5 %multiply_convert_fusion.3 = (bf16[512,3072]{1,0:T(8,128)(2,1)S(1)}, f32[512,3072]{1,0:T(8,128)}) fusion(f32[3072]{0:T(1024)S(1)} %copy-done.72, bf16[512,768]{1,0:T(8,128)(2,1)S(1)} %get-tuple-element.32, bf16[768,768]{1,0:T(8,128)(2,1)S(1)} %bitcast.230, bf16[768,768]{1,0:T(8,128)(2,1)S(1)} %bitcast.234, bf16[768,768]{1,0:T(8,128)(2,1)S(1)} %bitcast.238, ...), kind=kOutput, calls=%fused_computation.8 | convolution fusion | flops 2444230656 | bytes 14954496 | tf_op jit(solution)/shard_map/dot_general | solution.py:135
  239.1 2.7 fusion.130
  244.3 14.2 %fusion.119 = (f32[512]{0:T(512)S(1)}, f32[512]{0:T(512)S(1)}, f32[512,768]{1,0:T(8,128)}) fusion(f32[512,768]{1,0:T(8,128)} %copy-done.25, f32[768]{0:T(1024)S(1)} %copy-done.67, bf16[768,768]{1,0:T(8,128)(2,1)} %bitcast.229, bf16[768,768]{1,0:T(8,128)(2,1)} %bitcast.233, bf16[768,768]{1,0:T(8,128)(2,1)} %bitcast.237, bf16[768,768]{1,0:T(8,128)(2,1)} %bitcast.224, ...), kind=kOutput, calls=%fused_computation.226 | convolution fusion | flops 4877450240 | bytes 21266432 | tf_op jit(solution)/shard_map/dot_general | solution.py:63
  258.6 4.0 convolution_convert_fusion.14
  262.6 2.3 copy.51
  264.9 2.9 reshape.334
  267.8 2.3 fusion.45
  271.3 4.7 multiply_convert_fusion.1
  281.8 3.2 add_convert_fusion
  286.3 19.8 %collective-permute-done.1 = bf16[512,768]{1,0:T(8,128)(2,1)} collective-permute-done((bf16[512,768]{1,0:T(8,128)(2,1)}, bf16[512,768]{1,0:T(8,128)(2,1)}, u32[]{:S(2)}, u32[]{:S(2)}) %collective-permute-start.1) | collective-permute-done | bytes 786464 | tf_op jit(solution)/shard_map/ppermute | solution.py:15
  306.1 2.1 multiply_reduce_fusion
  308.2 1.9 fusion.120
  310.2 8.1 %fusion.123 = (bf16[3072]{0:T(1024)(128)(2,1)S(1)}, bf16[512,3072]{1,0:T(8,128)(2,1)S(1)}) fusion(f32[512,3072]{1,0:T(8,128)} %get-tuple-element.81, f32[3072]{0:T(1024)S(1)} %copy-done.72, bf16[3072,768]{1,0:T(8,128)(2,1)} %bitcast.193, f32[512,768]{1,0:T(8,128)S(1)} %get-tuple-element.29), kind=kOutput, calls=%fused_computation.230 | convolution fusion | flops 2435183616 | bytes 15747072 | tf_op jit(solution)/shard_map/dot_general | solution.py:63
  318.3 4.4 multiply_reduce_fusion.1
  324.3 1.7 convolution_convert_fusion.10
  326.0 2.5 copy.65
  328.5 2.9 reshape.338
  331.4 4.6 bitcast_convert_fusion
  337.6 2.8 multiply_convert_fusion
  349.3 1.8 convolution_convert_fusion.7
  351.1 1.8 convolution_convert_fusion.6
  356.6 2.4 constant_dynamic-update-slice_fusion.3
  363.2 2.1 convolution_convert_fusion.4
  373.6 2.9 convolution_convert_fusion
  376.6 2.6 constant_dynamic-update-slice_fusion.5
  381.1 6.1 %add_select_fusion = f32[512,768]{1,0:T(8,128)} fusion(f32[512,768]{1,0:T(8,128)S(1)} %copy-done.23, bf16[512,768]{0,1:T(8,128)(2,1)} %bitcast.248, bf16[512,768]{0,1:T(8,128)(2,1)} %bitcast.250, bf16[512,768]{0,1:T(8,128)(2,1)} %bitcast.252, f32[768]{0:T(1024)S(1)} %copy-done.70, f32[768]{0:T(1024)S(1)} %get-tuple-element.57, pred[]{:T(512)S(6)} %eq.3, ...), kind=kOutput, calls=%fused_computation.69 | convolution fusion | flops 1831993344 | bytes 10627073 | tf_op jit(solution)/shard_map/dot_general | solution.py:63
  387.3 50.0 %reduce-scatter.3.cloned.1.call-done = bf16[1,208,768]{2,1,0:T(8,128)(2,1)} async-done(((bf16[16,208,768]{2,1,0:T(8,128)(2,1)}), bf16[1,208,768]{2,1,0:T(8,128)(2,1)}) %reduce-scatter.3.cloned.1.call-update) | async-done | bytes 319504 | tf_op jit(solution)/shard_map/reduce_scatter | solution.py:250
  438.9 1.6 slice.267
  441.3 110.9 %reduce-scatter.5.cloned.1.call-done = bf16[1,384,768]{2,1,0:T(8,128)(2,1)} async-done(((bf16[16,384,768]{2,1,0:T(8,128)(2,1)}), bf16[1,384,768]{2,1,0:T(8,128)(2,1)}) %reduce-scatter.5.cloned.1.call-update) | async-done | bytes 589840 | tf_op jit(solution)/shard_map/reduce_scatter | solution.py:250
  (298 shorter events, 82.3 us)
Async XLA Ops:
  7.2 8.2 %copy-start.75 = (bf16[1,576]{1,0:T(2,128)(2,1)S(1)}, bf16[1,576]{1,0:T(2,128)(2,1)}, u32[]{:S(2)}) copy-start(bf16[1,576]{1,0:T(2,128)(2,1)} %param.13) | copy-start | bytes 3460
  7.2 9.2 %copy-start.77 = (s32[2,1]{0,1:T(1,128)S(1)}, s32[2,1]{0,1:T(1,128)}, u32[]{:S(2)}) copy-start(s32[2,1]{0,1:T(1,128)} %param.8) | copy-start | bytes 28
  7.2 125.0 %all-gather.3.cloned.1.call-start = ((), (), s32[]{:S(2)}) async-start(), calls=%async_computation.4 | async-start | bytes 15458304 | tf_op jit(solution)/shard_map/all_gather | solution.py:242
  16.3 421.0 %reduce-scatter.3.cloned.1.call-start = ((), (), s32[]{:S(2)}) async-start(), calls=%async_computation.2 | async-start | bytes 5431296 | tf_op jit(solution)/shard_map/reduce_scatter | solution.py:250
  138.8 11.6 %copy-start.65 = (f32[768]{0:T(1024)}, f32[768]{0:T(1024)S(1)}, u32[]{:S(2)}) copy-start(f32[768]{0:T(1024)S(1)} %get-tuple-element.64) | copy-start | bytes 9220
  139.4 6.5 %copy-start.6 = (bf16[1,2,1,256,768]{4,3,2,1,0:T(8,128)(2,1)S(1)}, bf16[1,2,1,256,768]{4,3,2,1,0:T(8,128)(2,1)}, u32[]{:S(2)}) copy-start(bf16[1,2,1,256,768]{4,3,2,1,0:T(8,128)(2,1)} %param.7) | copy-start | bytes 2359300
  157.4 2.6 copy-start.5
  179.7 22.2 %copy-start.44 = (bf16[16,48,768]{2,1,0:T(8,128)(2,1)S(1)}, bf16[16,48,768]{2,1,0:T(8,128)(2,1)}, u32[]{:S(2)}) copy-start(bf16[16,48,768]{2,1,0:T(8,128)(2,1)} %copy-done.43) | copy-start | bytes 3538948
  180.9 20.9 %collective-permute-start = (bf16[512,768]{1,0:T(8,128)(2,1)}, bf16[512,768]{1,0:T(8,128)(2,1)S(1)}, u32[]{:S(2)}, u32[]{:S(2)}) collective-permute-start(bf16[512,768]{1,0:T(8,128)(2,1)} %add_convert_fusion.3), channel_id=1, source_target_pairs={{0,16},{1,17},{2,18},{3,19},{4,20},{5,21},{6,22},{7,23},{8,24},{9,... | collective-permute-start | bytes 2359304 | tf_op jit(solution)/shard_map/ppermute | solution.py:15
  185.8 16.1 %copy-start.38 = (bf16[16,48,768]{2,1,0:T(8,128)(2,1)S(1)}, bf16[16,48,768]{2,1,0:T(8,128)(2,1)}, u32[]{:S(2)}) copy-start(bf16[16,48,768]{2,1,0:T(8,128)(2,1)} %copy-done.37) | copy-start | bytes 3538948
  185.8 16.1 %copy-start.41 = (bf16[16,48,768]{2,1,0:T(8,128)(2,1)S(1)}, bf16[16,48,768]{2,1,0:T(8,128)(2,1)}, u32[]{:S(2)}) copy-start(bf16[16,48,768]{2,1,0:T(8,128)(2,1)} %copy-done.40) | copy-start | bytes 3538948
  205.9 8.2 %copy-start.11 = (bf16[2,256,12,64]{1,0,3,2:T(2,128)(2,1)}, bf16[2,256,12,64]{1,0,3,2:T(2,128)(2,1)S(1)}, u32[]{:S(2)}) copy-start(bf16[2,256,12,64]{1,0,3,2:T(2,128)(2,1)S(1)} %reshape.333) | copy-start | bytes 2359300
  215.7 2.7 copy-start
  219.8 48.0 %copy-start.1 = (bf16[2,12,256,256]{2,3,1,0:T(8,128)(2,1)}, bf16[2,12,256,256]{2,3,1,0:T(8,128)(2,1)S(1)}, u32[]{:S(2)}) copy-start(bf16[2,12,256,256]{2,3,1,0:T(8,128)(2,1)S(1)} %fusion.6) | copy-start | bytes 9437188
  228.5 3.0 copy-start.56
  228.5 3.0 copy-start.72
  229.1 10.0 %slice-start.2 = ((s8[4718592]{0:T(1024)(128)(4,1)}), s8[4194304]{0:T(1024)(128)(4,1)S(1)}, s32[]{:S(2)}) async-start(s8[4718592]{0:T(1024)(128)(4,1)} %bitcast.194), calls=%async_computation.7 | async-start | bytes 8388608
  229.5 9.5 %copy-start.60 = (bf16[512,768]{1,0:T(8,128)(2,1)}, bf16[512,768]{1,0:T(8,128)(2,1)S(1)}, u32[]{:S(2)}) copy-start(bf16[512,768]{1,0:T(8,128)(2,1)S(1)} %get-tuple-element.32) | copy-start | bytes 2359300
  229.6 9.5 %copy-start.25 = (f32[512,768]{1,0:T(8,128)}, f32[512,768]{1,0:T(8,128)S(1)}, u32[]{:S(2)}) copy-start(f32[512,768]{1,0:T(8,128)S(1)} %get-tuple-element.33) | copy-start | bytes 4718596
  231.5 7.6 %slice-start.3 = ((s8[4718592]{0:T(1024)(128)(4,1)}), s8[524288]{0:T(1024)(128)(4,1)S(1)}, s32[]{:S(2)}) async-start(s8[4718592]{0:T(1024)(128)(4,1)} %bitcast.194), calls=%async_computation.8 | async-start | bytes 1048576
  231.5 7.6 %copy-start.74 = (f32[768]{0:T(1024)S(1)}, f32[768]{0:T(1024)}, u32[]{:S(2)}) copy-start(f32[768]{0:T(1024)} %get-tuple-element.59) | copy-start | bytes 9220
  239.1 2.8 copy-start.81
  241.9 2.4 copy-start.2
  267.8 2.4 copy-start.9
  267.8 2.4 copy-start.20
  271.3 4.7 copy-start.14
  278.6 2.2 copy-start.78
  281.8 24.3 %copy-start.3 = (f32[512,768]{1,0:T(8,128)S(1)}, f32[512,768]{1,0:T(8,128)}, u32[]{:S(2)}) copy-start(f32[512,768]{1,0:T(8,128)} %copy-done.2) | copy-start | bytes 4718596
  281.8 24.3 %copy-start.8 = (bf16[1,2,1,256,768]{4,3,2,1,0:T(8,128)(2,1)S(1)}, bf16[1,2,1,256,768]{4,3,2,1,0:T(8,128)(2,1)}, u32[]{:S(2)}) copy-start(bf16[1,2,1,256,768]{4,3,2,1,0:T(8,128)(2,1)} %param.7) | copy-start | bytes 2359300
  285.0 21.1 %collective-permute-start.1 = (bf16[512,768]{1,0:T(8,128)(2,1)}, bf16[512,768]{1,0:T(8,128)(2,1)}, u32[]{:S(2)}, u32[]{:S(2)}) collective-permute-start(bf16[512,768]{1,0:T(8,128)(2,1)} %add_convert_fusion), channel_id=1, source_target_pairs={{16,0},{17,1},{18,2},{19,3},{20,4},{21,5},{22,6},{23,7},{24,8},{25... | collective-permute-start | bytes 2359304 | tf_op jit(solution)/shard_map/ppermute | solution.py:15
  310.1 8.2 %copy-start.34 = (f32[512,768]{1,0:T(8,128)}, f32[512,768]{1,0:T(8,128)S(1)}, u32[]{:S(2)}) copy-start(f32[512,768]{1,0:T(8,128)S(1)} %get-tuple-element.29) | copy-start | bytes 4718596
  310.1 8.2 %copy-start.27 = (f32[512,768]{1,0:T(8,128)S(1)}, f32[512,768]{1,0:T(8,128)}, u32[]{:S(2)}) copy-start(f32[512,768]{1,0:T(8,128)} %copy-done.25) | copy-start | bytes 4718596
  310.1 8.2 %copy-start.51 = (bf16[16,48,768]{2,1,0:T(8,128)(2,1)S(1)}, bf16[16,48,768]{2,1,0:T(8,128)(2,1)}, u32[]{:S(2)}) copy-start(bf16[16,48,768]{2,1,0:T(8,128)(2,1)} %get-tuple-element.34) | copy-start | bytes 3538948
  310.1 8.2 %copy-start.53 = (bf16[16,48,768]{2,1,0:T(8,128)(2,1)S(1)}, bf16[16,48,768]{2,1,0:T(8,128)(2,1)}, u32[]{:S(2)}) copy-start(bf16[16,48,768]{2,1,0:T(8,128)(2,1)} %get-tuple-element.35) | copy-start | bytes 3538948
  310.2 8.2 %copy-start.55 = (bf16[16,48,768]{2,1,0:T(8,128)(2,1)S(1)}, bf16[16,48,768]{2,1,0:T(8,128)(2,1)}, u32[]{:S(2)}) copy-start(bf16[16,48,768]{2,1,0:T(8,128)(2,1)} %get-tuple-element.36) | copy-start | bytes 3538948
  310.2 8.2 %copy-start.57 = (bf16[16,48,768]{2,1,0:T(8,128)(2,1)S(1)}, bf16[16,48,768]{2,1,0:T(8,128)(2,1)}, u32[]{:S(2)}) copy-start(bf16[16,48,768]{2,1,0:T(8,128)(2,1)} %get-tuple-element.37) | copy-start | bytes 3538948
  318.3 4.4 copy-start.79
  326.0 11.5 %slice-start = ((s8[6291456]{0:T(1024)(128)(4,1)}), s8[2097152]{0:T(1024)(128)(4,1)S(1)}, s32[]{:S(2)}) async-start(s8[6291456]{0:T(1024)(128)(4,1)} %bitcast.182), calls=%async_computation.5 | async-start | bytes 4194304
  331.4 4.6 copy-start.10
  331.4 6.1 %slice-start.1 = ((s8[6291456]{0:T(1024)(128)(4,1)}), s8[4194304]{0:T(1024)(128)(4,1)S(1)}, s32[]{:S(2)}) async-start(s8[6291456]{0:T(1024)(128)(4,1)} %bitcast.182), calls=%async_computation.6 | async-start | bytes 8388608
  337.6 2.8 copy-start.15
  344.9 6.2 %copy-start.62 = (bf16[96,8,2,256]{3,1,2,0:T(8,128)(2,1)}, bf16[96,8,2,256]{3,1,2,0:T(8,128)(2,1)S(1)}, u32[]{:S(2)}) copy-start(bf16[96,8,2,256]{3,1,2,0:T(8,128)(2,1)S(1)} %copy.103) | copy-start | bytes 2359300
  345.9 3.4 copy-start.63
  354.6 4.5 copy-start.58
  362.1 190.1 %reduce-scatter.5.cloned.1.call-start = ((), (), s32[]{:S(2)}) async-start(), calls=%async_computation.3 | async-start | bytes 10027008 | tf_op jit(solution)/shard_map/reduce_scatter | solution.py:250
  363.2 3.2 copy-start.80
  370.4 2.5 copy-start.82
  371.2 2.4 copy-start.35
  (44 other events, 67.0 us)
Sparse Core Ops, SparseCore 0:
  16.4 115.7 all-gather.2
  362.3 74.9 reduce-scatter.2
  442.0 110.2 reduce-scatter.4
